TPU v7x, 256 devices: a whole 4x4x8 slice. The times are simulated.
256 devices in a mesh: row: 32 (over y, x, z_lo), col: 8 (over z_hi, core).
Axes of the slice: x: 4, y: 4, z: 8 (z_hi: 4, z_lo: 2; z = z_hi * 2 + z_lo), core: 2. Of those that a mesh axis runs over, the one named last changes fastest.
Arguments:
- feature_codes: int32 [131072, 256], P(('row', 'col')), may hold values from -127 to 127
- bit_widths: int32 [256], P(('row', 'col')), may hold values from 4 to 8
- row_scales: float32 [131072], P(('row', 'col')), may hold values from 0.003 to 0.03
- weight: bfloat16 [256, 256], P('col'), may hold values from -0.375 to 0.375
- layer_bias: float32 [256], replicated, may hold values from -3 to 3
- adjacency_blocks: bfloat16 [1024, 8, 11, 128, 128], P('row', 'col'), may hold values from 0.0049743652 to 0.099609375
- block_index: int32 [1024, 8, 11], P('row', 'col'), may hold values from 0 to 127
- block_counts: int32 [1024, 8], P('row', 'col'), may hold values from 1 to 11, as said below
Outputs:
- aggregated: bfloat16 [131072, 256], P(('row', 'col'))
Inputs may be any that keep to these rules, and one draw needn't show every extreme that they name: `block_index`: column blocks within a column group. `block_counts`: row blocks of one device may differ in live slots; some row block uses all 11.
All inputs are finite; a program needn't handle non-finite values.
Results may differ from a plain program's by a relative error of at most 0.0041.
Values may be sent and summed in bfloat16 or wider, within the bound.
No kernel may reach another device: no remote copies, remote signals or barrier semaphores. Data moves between devices by JAX's collectives and lax.ppermute only.
A program may use at most 128 MiB of HBM per device.

v0:
```python
import jax
import jax.numpy as jnp
from jax import lax
from jax.sharding import PartitionSpec as P


def on_device(
    feature_codes,
    bit_widths,
    row_scales,
    weight,
    layer_bias,
    adjacency_blocks,
    block_index,
    block_counts,
):
    unit = jnp.left_shift(jnp.ones_like(bit_widths), 8 - bit_widths)
    level = jnp.floor_divide(feature_codes, unit[0]) * unit[0]
    features = (level.astype(jnp.float32) * row_scales[:, None]).astype(jnp.bfloat16)
    full_weight = lax.all_gather(weight, "col", axis=0, tiled=True)
    source = jnp.dot(features, full_weight, preferred_element_type=jnp.float32).astype(jnp.bfloat16)
    feat_width = source.shape[1]
    group_rows = lax.all_gather(source, "row", axis=0, tiled=True)
    blocks_here = adjacency_blocks[:, 0]
    index_here = block_index[:, 0]
    row_blocks = blocks_here.shape[0]
    block_size = blocks_here.shape[-1]
    slot_ids = jnp.arange(index_here.shape[1], dtype=jnp.int32)
    live_mask = slot_ids[None, :] < block_counts[:, 0][:, None]
    blocks_live = jnp.where(live_mask[:, :, None, None], blocks_here, jnp.zeros_like(blocks_here))
    column_blocks = group_rows.reshape(group_rows.shape[0] // block_size, block_size, feat_width)
    picked = column_blocks[index_here]
    running = jnp.einsum("rmij,rmjf->rif", blocks_live, picked, preferred_element_type=jnp.float32)
    partial_value = running.reshape(row_blocks * block_size, feat_width)
    summed = lax.psum_scatter(partial_value, "col", scatter_dimension=0, tiled=True)
    return jnp.maximum(summed + layer_bias[None, :], 0.0).astype(jnp.bfloat16)


def solution(mesh):
    in_specs = (
        P(("row", "col"), None),
        P(("row", "col")),
        P(("row", "col")),
        P("col", None),
        P(),
        P("row", "col", None, None, None),
        P("row", "col", None),
        P("row", "col"),
    )
    out_specs = P(("row", "col"), None)
    return jax.shard_map(
        on_device, mesh=mesh, in_specs=in_specs, out_specs=out_specs, check_vma=False
    )
```

profile of v0, /device:TPU:38, one launch (start us, length us, event | category | flops | bytes accessed | tf_op | source)
XLA Modules:
  0.0 318.4 jit_solution(10943070377025459209)
XLA Ops:
  6.5 0.0 all-gather.2.cloned.1.call-start
  7.2 17.5 %all_gather.6 = bf16[256,256]{1,0:T(8,128)(2,1)S(1)} all-gather(bf16[32,256]{1,0:T(8,128)(2,1)} %param.11), channel_id=1, replica_groups=mesh['row'=32,'col'=8] {'col'}, dimensions={0}, use_global_device_ids=true | all-gather | bytes 147456 | tf_op jit(solution)/shard_map/all_gather | solution.py:20
  24.7 7.0 %convolution_convert_fusion = bf16[512,256]{1,0:T(8,128)(2,1)} fusion(bf16[256,256]{1,0:T(8,128)(2,1)S(1)} %all_gather.6, s32[512,256]{1,0:T(8,128)} %param.8, f32[512]{0:T(512)} %param.10, s32[]{:T(128)} %bitcast.2, s32[]{:T(128)S(6)} %sign.9), kind=kOutput, calls=%fused_computation.5 | convolution fusion | flops 68812800 | bytes 919560 | tf_op jit(solution)/shard_map/dot_general | solution.py:21
  31.7 0.0 all-gather.2.cloned.1.call-update
  31.7 0.0 reduce-scatter.2.cloned.1.call-start
  31.8 0.7 compare_select_fusion
  32.5 0.1 copy.9
  32.6 0.1 reshape.62
  32.7 0.7 iota_compare_fusion
  33.4 187.1 %all-gather.2.cloned.1.call-done = bf16[16384,256]{1,0:T(8,128)(2,1)} async-done(((bf16[512,256]{1,0:T(8,128)(2,1)}), bf16[16384,256]{1,0:T(8,128)(2,1)}) %all-gather.2.cloned.1.call-update) | async-done | bytes 8388624 | tf_op jit(solution)/shard_map/all_gather | solution.py:23
  220.5 15.7 %gather_fusion = bf16[352,128,256]{2,1,0:T(8,128)(2,1)} fusion(bf16[128,128,256]{2,1,0:T(8,128)(2,1)} %bitcast.17, s32[1024]{0:T(1024)S(1)} %pad_clamp_fusion), kind=kCustom, calls=%fused_computation | custom fusion | bytes 46138752 | tf_op jit(solution)/shard_map/gather | solution.py:32
  236.2 0.0 copy-start
  236.2 14.9 %fusion = f32[32,128,256,1]{2,1,3,0:T(8,128)} fusion(bf16[32,11,128,256]{3,2,1,0:T(8,128)(2,1)} %bitcast.18, bf16[32,1,11,128,128]{4,3,2,1,0:T(8,128)(2,1)} %param.13, pred[32,11]{1,0:T(8,128)(4,1)S(1)} %iota_compare_fusion), kind=kOutput, calls=%fused_computation.2 | convolution fusion | flops 2958557184 | bytes 38797664 | tf_op jit(solution)/shard_map/rmij,rmjf->rif/dot_general | solution.py:33
  251.1 0.0 reduce-scatter.2.cloned.1.call-update
  251.1 58.6 %reduce-scatter.2.cloned.1.call-done = f32[512,256]{1,0:T(8,128)} async-done(((f32[4096,256]{1,0:T(8,128)}), f32[512,256]{1,0:T(8,128)}) %reduce-scatter.2.cloned.1.call-update) | async-done | bytes 524304 | tf_op jit(solution)/shard_map/reduce_scatter | solution.py:35
  309.7 0.0 copy-done
  309.7 1.8 maximum_convert_fusion
  (1 shorter events, 0.0 us)
Async XLA Ops:
  6.5 214.0 %all-gather.2.cloned.1.call-start = ((), (), s32[]{:S(2)}) async-start(), calls=%async_computation.1 | async-start | bytes 8650752 | tf_op jit(solution)/shard_map/all_gather | solution.py:23
  31.7 278.0 %reduce-scatter.2.cloned.1.call-start = ((), (), s32[]{:S(2)}) async-start(), calls=%async_computation.2 | async-start | bytes 4718592 | tf_op jit(solution)/shard_map/reduce_scatter | solution.py:35
  236.2 73.5 %copy-start = (f32[256]{0:T(256)S(1)}, f32[256]{0:T(256)}, u32[]{:S(2)}) copy-start(f32[256]{0:T(256)} %param.12) | copy-start | bytes 3076
Sparse Core Ops, SparseCore 0:
  31.9 188.6 all-gather.1
  251.2 58.4 reduce-scatter.1
where the time goes:
time: 322 us; the launch traced here: 318 us
  waiting for transfers between devices  246 us (76%)
  matrix products  21.9 us (7%)
  blocking collectives  17.5 us (5%)
  local copies, waits for them, and re-layouts  15.9 us (5%)
  between operations  14.1 us (4%)
  other arithmetic  3.23 us (1%)
    all_gather x1, waiting for transfers between devices, on_device(): group_rows = lax.all_gather(source, 'row', axis=0, tiled=True)  187 us
    reduce_scatter x1, waiting for transfers between devices, on_device(): lax.psum_scatter(partial_value, 'col', scatter_dimension=0, tiled=True)  58.6 us
    all_gather x1, blocking collectives, on_device(): full_weight = lax.all_gather(weight, 'col', axis=0, tiled=True)  17.5 us
    gather x1, local copies, waits for them, and re-layouts, on_device(): picked = column_blocks[index_here]  15.7 us
    dot_general x1, matrix products, on_device(): jnp.einsum('rmij,rmjf->rif', blocks_live, picked, preferred_element_type=...  14.9 us
    dot_general x1, matrix products, on_device(): jnp.dot(features, full_weight, preferred_element_type=jnp.float32)  7.03 us
  transfers between devices with their start and end apart: 2, of which 2 were waited for; matrix products, arithmetic and copies ran while one was open for 1% of the time, Pallas kernels for 0%

commit v1 on v0

v1 whole, which is shorter than its diff:
```python
import functools

import jax
import jax.numpy as jnp
from jax import lax
from jax.experimental import pallas as pl
from jax.experimental.pallas import tpu as pltpu
from jax.sharding import PartitionSpec as P

NX, NY, NZ = 4, 4, 2
NH = 4
PANEL = 512
BLOCK = 128
F = 256
RB = 32
MAXB = 11
KPER = PANEL // BLOCK
SHARDS = NX * NY * NZ
ADJ_COPIES = 4
TILE = 6
KERNEL_VMEM = 24 << 20

PLAN = (
    (1, 1, ((0, 0, 0),)),
    (0, -1, ((0, 0, 0),)),
    (2, 1, ((0, 0, 0),)),
    (0, 1, ((0, 0, 0),)),
    (1, -1, ((0, 0, 0),)),
    (1, 1, ((0, 1, 0),)),
    (0, -1, ((3, 0, 0),)),
    (2, 1, ((3, 0, 0), (0, 1, 0))),
    (0, 1, ((0, 0, 1),)),
    (1, -1, ((3, 0, 0),)),
    (1, 1, ((3, 0, 0), (1, 0, 0))),
    (0, -1, ((0, 2, 0),)),
    (0, 1, ((1, 0, 1),)),
    (1, -1, ((1, 0, 1), (2, 0, 0), (1, 0, 0))),
    (2, 1, ((0, 2, 0),)),
    (0, -1, ((3, 2, 0),)),
    (0, 1, ((0, 2, 0), (0, 1, 1))),
    (1, 1, ((2, 0, 0), (3, 0, 1), (2, 0, 1))),
    (2, 1, ((0, 3, 0),)),
    (0, -1, ((0, 2, 1),)),
    (2, 1, ((3, 3, 0),)),
    (0, -1, ((3, 2, 1),)),
    (0, 1, ((0, 2, 1),)),
    (1, -1, ((2, 0, 1),)),
)
LATE = (17, 20, 21, 22, 23)
WEIGHT_AFTER = (5, 10)


def row_perm(axis, step):
    pairs = []
    for y in range(NY):
        for x in range(NX):
            for z in range(NZ):
                c = [x, y, z]
                c[axis] = (c[axis] + step) % (NX, NY, NZ)[axis]
                pairs.append(((y * NX + x) * NZ + z, (c[1] * NX + c[0]) * NZ + c[2]))
    return pairs


def col_perm(dz, core):
    return [(h * 2 + c, ((h + dz) % NH) * 2 + (c ^ core)) for h in range(NH) for c in range(2)]


def after(value, *others):
    return lax.optimization_barrier((value, *others))[0]


def moved(place, axis, step):
    place = list(place)
    place[axis] = (place[axis] + step) % (NX, NY, NZ)[axis]
    return tuple(place)


def gather_rows(mine):
    arrays, at, last = [(mine, ((0, 0, 0),))], {(0, 0, 0): (0, 0)}, {}
    for axis, step, sources in PLAN:
        index = at[sources[0]][0]
        if arrays[index][1] == sources:
            value = arrays[index][0]
        else:
            rows = []
            for source in sources:
                index, n = at[source]
                array = arrays[index][0]
                rows.append(array if len(arrays[index][1]) == 1 else array[n * PANEL : (n + 1) * PANEL])
            value = rows[0] if len(rows) == 1 else jnp.concatenate(rows)
        link = (axis, step)
        if link in last:
            value = after(value, last[link])
        last[link] = got = lax.ppermute(value, "row", row_perm(axis, step))
        places = tuple(moved(source, axis, step) for source in sources)
        for n, place in enumerate(places):
            at[place] = (len(arrays), n)
        arrays.append((got, places))
    return arrays


def gather_weight(weight, arrays):
    pair = jnp.concatenate([weight, lax.ppermute(weight, "col", col_perm(0, 1))])
    pair = after(pair, arrays[1 + WEIGHT_AFTER[0]][0])
    quad = jnp.concatenate([pair, lax.ppermute(pair, "col", col_perm(1, 0))])
    quad = after(quad, arrays[1 + WEIGHT_AFTER[1]][0])
    whole = jnp.concatenate([quad, lax.ppermute(quad, "col", col_perm(2, 0))])
    return whole.reshape(NH * 2, F // (NH * 2), F)


def lay_weight(here_ref, weight_ref, weight):
    col = here_ref[1]
    rows = F // (NH * 2)
    for n in range(NH * 2):
        place = ((lax.shift_right_logical(col, 1) - n // 2) & (NH - 1)) * 2 + ((col & 1) ^ (n % 2))
        weight[pl.ds(pl.multiple_of(place * rows, rows), rows), :] = weight_ref[n]


def copies_of(refs, places, target, sems):
    copies, at = [], 0
    for n, ref in enumerate(refs):
        rows = len(places[n]) * PANEL
        copies.append(pltpu.make_async_copy(ref, target.at[pl.ds(at, rows)], sems.at[n]))
        at += rows
    return copies


def early_kernel(places, here_ref, weight_ref, adj_hbm, *refs):
    pieces = refs[: len(places)]
    hidden, adj, weight, adj_sems, sems = refs[len(places) :]
    copies = copies_of(pieces, places, hidden, sems)
    part = RB // ADJ_COPIES
    adj_copies = [
        pltpu.make_async_copy(adj_hbm.at[pl.ds(n * part, part), 0], adj.at[pl.ds(n * part, part)], adj_sems.at[n])
        for n in range(ADJ_COPIES)
    ]
    for copy in copies:
        copy.start()
    for copy in adj_copies:
        copy.start()
    lay_weight(here_ref, weight_ref, weight)
    hidden[pl.ds(SHARDS * PANEL, BLOCK), :] = jnp.zeros((BLOCK, F), jnp.bfloat16)
    total, ready, done = sum(len(p) for p in places), 0, 0
    for n, copy in enumerate(copies):
        copy.wait()
        ready += len(places[n])
        if ready - done >= TILE or ready == total:
            at = pl.ds(done * PANEL, (ready - done) * PANEL)
            hidden[at, :] = jnp.dot(
                hidden[at, :], weight[...], preferred_element_type=jnp.float32
            ).astype(jnp.bfloat16)
            done = ready
    for copy in adj_copies:
        copy.wait()


def early(here, weight_rows, adjacency, pieces, places):
    smem, vmem, anywhere = (pl.BlockSpec(memory_space=m) for m in (pltpu.SMEM, pltpu.VMEM, pl.ANY))
    return pl.pallas_call(
        functools.partial(early_kernel, places),
        in_specs=[smem, vmem, anywhere] + [anywhere] * len(pieces),
        out_specs=[vmem, vmem],
        scratch_shapes=[
            pltpu.VMEM((F, F), jnp.bfloat16),
            pltpu.SemaphoreType.DMA((ADJ_COPIES,)),
            pltpu.SemaphoreType.DMA((len(pieces),)),
        ],
        out_shape=[
            pltpu.VMEM((SHARDS * PANEL + BLOCK, F), jnp.bfloat16),
            pltpu.VMEM((RB, MAXB, BLOCK, BLOCK), jnp.bfloat16),
        ],
        compiler_params=pltpu.CompilerParams(vmem_limit_bytes=KERNEL_VMEM),
        cost_estimate=pl.CostEstimate(flops=2 * 13000 * F * F, bytes_accessed=20 << 20, transcendentals=0),
    )(here, weight_rows, adjacency, *pieces)


def late_kernel(places, before, here_ref, index_ref, count_ref, weight_ref, hidden_in, adj_in, *refs):
    pieces = refs[: len(places)]
    send_ref, keep_ref, hidden, adj, weight, table = refs[len(places) :]
    del hidden_in, adj_in
    lay_weight(here_ref, weight_ref, weight)
    row, col = here_ref[0], here_ref[1]
    y, x, z = lax.shift_right_logical(row, 3), lax.shift_right_logical(row, 1) & (NX - 1), row & (NZ - 1)
    order = [place for group in before + places for place in group]
    for n, (dx, dy, dz) in enumerate(order):
        shard = (((y - dy) & (NY - 1)) * NX + ((x - dx) & (NX - 1))) * NZ + (z ^ dz)
        table[shard] = n * PANEL
    at = sum(len(p) for p in before) * PANEL
    for piece in pieces:
        rows = pl.ds(at, piece.shape[0])
        hidden[rows, :] = jnp.dot(piece[...], weight[...], preferred_element_type=jnp.float32).astype(jnp.bfloat16)
        at += piece.shape[0]
    chip, core = lax.shift_right_logical(col, 1), col & 1

    def rows_at(block, m):
        column = index_ref[block, 0, m]
        start = table[lax.shift_right_logical(column, 2)] + (column & (KPER - 1)) * BLOCK
        start = jnp.where(m < count_ref[block, 0], start, SHARDS * PANEL)
        return hidden[pl.ds(pl.multiple_of(start, BLOCK), BLOCK), :]

    def total_of(block):
        right = [rows_at(block, m) for m in range(MAXB)]
        left = [adj[block, m] for m in range(MAXB)]
        return jnp.dot(
            jnp.concatenate(left, axis=1), jnp.concatenate(right, axis=0), preferred_element_type=jnp.float32
        )

    def panels(side, out_ref):
        def body(d, _):
            panel = ((chip + d) & (NH - 1)) * 2 + side
            for j in range(KPER):
                at = pl.ds(pl.multiple_of(d * PANEL + j * BLOCK, BLOCK), BLOCK)
                out_ref[at, :] = total_of(panel * KPER + j).astype(out_ref.dtype)
            return 0

        lax.fori_loop(0, NH, body, 0)

    panels(core ^ 1, send_ref)
    panels(core, keep_ref)


def late(here, index, counts, weight_rows, hidden, adj, pieces, places, before):
    smem, vmem = (pl.BlockSpec(memory_space=m) for m in (pltpu.SMEM, pltpu.VMEM))
    return pl.pallas_call(
        functools.partial(late_kernel, places, before),
        in_specs=[smem, smem, smem, vmem, vmem, vmem] + [vmem] * len(pieces),
        out_specs=[vmem, vmem, vmem, vmem],
        scratch_shapes=[
            pltpu.VMEM((F, F), jnp.bfloat16),
            pltpu.SMEM((SHARDS,), jnp.int32),
        ],
        out_shape=[
            pltpu.VMEM((NH * PANEL, F), jnp.bfloat16),
            pltpu.VMEM((NH * PANEL, F), jnp.float32),
            pltpu.VMEM((SHARDS * PANEL + BLOCK, F), jnp.bfloat16),
            pltpu.VMEM((RB, MAXB, BLOCK, BLOCK), jnp.bfloat16),
        ],
        input_output_aliases={4: 2, 5: 3},
        compiler_params=pltpu.CompilerParams(vmem_limit_bytes=KERNEL_VMEM),
    )(here, index, counts, weight_rows, hidden, adj, *pieces)


def reduce_chips(send, keep):
    got = lax.ppermute(send, "col", col_perm(0, 1))
    h = PANEL // 2

    def part(d, side):
        at = d * PANEL + side * h
        return keep[at : at + h] + got[at : at + h].astype(jnp.float32)

    def plus(value):
        return lax.ppermute(value.astype(jnp.bfloat16), "col", col_perm(1, 0)).astype(jnp.float32)

    def minus(value):
        return lax.ppermute(value.astype(jnp.bfloat16), "col", col_perm(-1, 0)).astype(jnp.float32)

    first = [part(2, 0), part(2, 1), part(1, 1), part(3, 0)]
    first = lax.optimization_barrier([value.astype(jnp.bfloat16) for value in first])
    far_top, far_bottom = plus(first[0]), minus(first[1])
    near_bottom, near_top = plus(first[2]), minus(first[3])
    chain_top = plus(part(1, 0) + far_top)
    chain_bottom = minus(part(3, 1) + far_bottom)
    top = part(0, 0) + near_top + chain_top
    bottom = part(0, 1) + near_bottom + chain_bottom
    return jnp.concatenate([top, bottom])


def on_device(
    feature_codes,
    bit_widths,
    row_scales,
    weight,
    layer_bias,
    adjacency_blocks,
    block_index,
    block_counts,
):
    here = jnp.stack([lax.axis_index("row"), lax.axis_index("col")]).astype(jnp.int32)
    shift = 8 - bit_widths[0]
    level = jnp.left_shift(jnp.right_shift(feature_codes, shift), shift)
    features = (level.astype(jnp.float32) * row_scales[:, None]).astype(jnp.bfloat16)
    arrays = gather_rows(features)
    weight_rows = gather_weight(weight, arrays)

    soon = [a for n, a in enumerate(arrays) if n - 1 not in LATE]
    last = [arrays[n + 1] for n in LATE]
    soon_places, last_places = [p for _, p in soon], [p for _, p in last]
    hidden, adj = early(here, weight_rows, adjacency_blocks, [a for a, _ in soon], soon_places)
    send, keep, _, _ = late(
        here, block_index, block_counts, weight_rows, hidden, adj, [a for a, _ in last], last_places, soon_places
    )
    summed = reduce_chips(send, keep)
    return jnp.maximum(summed + layer_bias[None, :], 0.0).astype(jnp.bfloat16)


def solution(mesh):
    in_specs = (
        P(("row", "col"), None),
        P(("row", "col")),
        P(("row", "col")),
        P("col", None),
        P(),
        P("row", "col", None, None, None),
        P("row", "col", None),
        P("row", "col"),
    )
    out_specs = P(("row", "col"), None)
    return jax.shard_map(
        on_device, mesh=mesh, in_specs=in_specs, out_specs=out_specs, check_vma=False
    )
```

time: 322 us -> 123 us (0.38)
  the two profiles are of different devices: /device:TPU:38 before, /device:TPU:6 now
where the time goes in v1:
time: 123 us
  waiting for transfers between devices  55.5 us (45%)
  starting transfers between devices  41 us (33%)
  Pallas kernels  13.4 us (11%)
  local copies, waits for them, and re-layouts  7.26 us (6%)
  other arithmetic  4.55 us (4%)
    ppermute x24, starting transfers between devices, gather_rows(): last[link] = got = lax.ppermute(value, 'row', row_perm(axis, step))  32.5 us
    ppermute x24, waiting for transfers between devices, gather_rows(): last[link] = got = lax.ppermute(value, 'row', row_perm(axis, step))  17.7 us
    ppermute x3, waiting for transfers between devices, plus(): lax.ppermute(value.astype(jnp.bfloat16), 'col', col_perm(1, 0))  15 us
    ppermute x1, waiting for transfers between devices, gather_weight(): quad = jnp.concatenate([pair, lax.ppermute(pair, 'col', col_perm(1, 0))])  9.73 us
    ppermute x3, waiting for transfers between devices, minus(): lax.ppermute(value.astype(jnp.bfloat16), 'col', col_perm(-1, 0))  9.29 us
    unnamed x30, local copies, waits for them, and re-layouts  7.22 us
    pallas_call x1, Pallas kernels, early(): pl.pallas_call(functools.partial(early_kernel, places), in_specs=[smem, v...  6.85 us
    pallas_call x1, Pallas kernels, late(): pl.pallas_call(functools.partial(late_kernel, places, before), in_specs=[...  6.54 us
  transfers between devices with their start and end apart: 34, of which 18 were waited for; matrix products, arithmetic and copies ran while one was open for 2% of the time, Pallas kernels for 6%

profile of v1, /device:TPU:6, one launch (start us, length us, event | category | flops | bytes accessed | tf_op | source)
XLA Modules:
  0.0 122.6 jit_solution(4223495359861589323)
XLA Ops:
  1.8 2.3 %collective-permute-start.5 = (bf16[512,256]{1,0:T(8,128)(2,1)S(1)}, bf16[512,256]{1,0:T(8,128)(2,1)S(1)}, u32[]{:S(2)}, u32[]{:S(2)}) collective-permute-start(bf16[512,256]{1,0:T(8,128)(2,1)S(1)} %multiply_convert_fusion.refs_0_), channel_id=1, source_target_pairs={{0,16},{8,24},{16,32},{24,40},{32,48},{40,56},{48,0},{56,8},{64,80... | collective-permute-start | bytes 786440 | tf_op jit(solution)/shard_map/ppermute | solution.py:94
  5.5 1.9 %collective-permute-start.8 = (bf16[512,256]{1,0:T(8,128)(2,1)S(1)}, bf16[512,256]{1,0:T(8,128)(2,1)S(1)}, u32[]{:S(2)}, u32[]{:S(2)}) collective-permute-start(bf16[512,256]{1,0:T(8,128)(2,1)S(1)} %multiply_convert_fusion.refs_0_), channel_id=1, source_target_pairs={{0,8},{8,0},{16,24},{24,16},{32,40},{40,32},{48,56},{56,48},{64,72... | collective-permute-start | bytes 786440 | tf_op jit(solution)/shard_map/ppermute | solution.py:94
  7.4 2.5 %collective-permute-done.5.refs_4_ = bf16[512,256]{1,0:T(8,128)(2,1)S(1)} collective-permute-done((bf16[512,256]{1,0:T(8,128)(2,1)S(1)}, bf16[512,256]{1,0:T(8,128)(2,1)S(1)}, u32[]{:S(2)}, u32[]{:S(2)}) %collective-permute-start.5) | collective-permute-done | bytes 262176 | tf_op jit(solution)/shard_map/ppermute | solution.py:94
  10.0 1.8 %collective-permute-done.4.refs_2_ = bf16[512,256]{1,0:T(8,128)(2,1)S(1)} collective-permute-done((bf16[512,256]{1,0:T(8,128)(2,1)S(1)}, bf16[512,256]{1,0:T(8,128)(2,1)S(1)}, u32[]{:S(2)}, u32[]{:S(2)}) %collective-permute-start.4) | collective-permute-done | bytes 262176 | tf_op jit(solution)/shard_map/ppermute | solution.py:94
  12.9 1.9 %collective-permute-start.11 = (bf16[1024,256]{1,0:T(8,128)(2,1)S(1)}, bf16[1024,256]{1,0:T(8,128)(2,1)S(1)}, u32[]{:S(2)}, u32[]{:S(2)}) collective-permute-start(bf16[1024,256]{1,0:T(8,128)(2,1)S(1)} %get-tuple-element.39), channel_id=1, source_target_pairs={{0,8},{8,0},{16,24},{24,16},{32,40},{40,32},{48,56},{56,48},{64,72... | collective-permute-start | bytes 1572872 | tf_op jit(solution)/shard_map/ppermute | solution.py:94
  17.2 1.7 %collective-permute-start.9 = (bf16[512,256]{1,0:T(8,128)(2,1)S(1)}, bf16[512,256]{1,0:T(8,128)(2,1)}, u32[]{:S(2)}, u32[]{:S(2)}) collective-permute-start(bf16[512,256]{1,0:T(8,128)(2,1)S(1)} %multiply_convert_fusion.refs_0_), channel_id=1, source_target_pairs={{0,192},{8,200},{16,208},{24,216},{32,224},{40,232},{48,240},{56,2... | collective-permute-start | bytes 786440 | tf_op jit(solution)/shard_map/ppermute | solution.py:94
  21.2 2.8 %collective-permute-start.15 = (bf16[512,256]{1,0:T(8,128)(2,1)S(1)}, bf16[512,256]{1,0:T(8,128)(2,1)S(1)}, u32[]{:S(2)}, u32[]{:S(2)}) collective-permute-start(bf16[512,256]{1,0:T(8,128)(2,1)S(1)} %collective-permute-done.12.refs_9_), channel_id=1, source_target_pairs={{0,16},{8,24},{16,32},{24,40},{32,48},{40,56},{48,0},{56,8},{64,80... | collective-permute-start | bytes 786440 | tf_op jit(solution)/shard_map/ppermute | solution.py:94
  24.1 2.5 %collective-permute-start.13 = (bf16[512,256]{1,0:T(8,128)(2,1)S(1)}, bf16[512,256]{1,0:T(8,128)(2,1)S(1)}, u32[]{:S(2)}, u32[]{:S(2)}) collective-permute-start(bf16[512,256]{1,0:T(8,128)(2,1)S(1)} %collective-permute-done.4.refs_2_), channel_id=1, source_target_pairs={{0,192},{8,200},{16,208},{24,216},{32,224},{40,232},{48,240},{56,2... | collective-permute-start | bytes 786440 | tf_op jit(solution)/shard_map/ppermute | solution.py:94
  29.2 2.3 %collective-permute-done.13.refs_10_ = bf16[512,256]{1,0:T(8,128)(2,1)S(1)} collective-permute-done((bf16[512,256]{1,0:T(8,128)(2,1)S(1)}, bf16[512,256]{1,0:T(8,128)(2,1)S(1)}, u32[]{:S(2)}, u32[]{:S(2)}) %collective-permute-start.13) | collective-permute-done | bytes 262176 | tf_op jit(solution)/shard_map/ppermute | solution.py:94
  31.5 3.1 %collective-permute-start.16 = (bf16[1536,256]{1,0:T(8,128)(2,1)}, bf16[1536,256]{1,0:T(8,128)(2,1)}, u32[]{:S(2)}, u32[]{:S(2)}) collective-permute-start(bf16[1536,256]{1,0:T(8,128)(2,1)} %get-tuple-element.44), channel_id=1, source_target_pairs={{0,192},{8,200},{16,208},{24,216},{32,224},{40,232},{48,240},{56,2... | collective-permute-start | bytes 2359304 | tf_op jit(solution)/shard_map/ppermute | solution.py:94
  36.7 3.2 %collective-permute-start.19 = (bf16[1024,256]{1,0:T(8,128)(2,1)}, bf16[1024,256]{1,0:T(8,128)(2,1)}, u32[]{:S(2)}, u32[]{:S(2)}) collective-permute-start(bf16[1024,256]{1,0:T(8,128)(2,1)} %pad_maximum_fusion.4), channel_id=1, source_target_pairs={{0,16},{8,24},{16,32},{24,40},{32,48},{40,56},{48,0},{56,8},{64,80... | collective-permute-start | bytes 1572872 | tf_op jit(solution)/shard_map/ppermute | solution.py:94
  44.2 2.7 %collective-permute-start.3 = (bf16[64,256]{1,0:T(8,128)(2,1)S(1)}, bf16[64,256]{1,0:T(8,128)(2,1)S(1)}, u32[]{:S(2)}, u32[]{:S(2)}) collective-permute-start(bf16[64,256]{1,0:T(8,128)(2,1)S(1)} %pad_maximum_fusion.7), channel_id=1, source_target_pairs={{0,2},{1,3},{2,4},{3,5},{4,6},{5,7},{6,0},{7,1},{8,10},{9,11},{10,... | collective-permute-start | bytes 98312 | tf_op jit(solution)/shard_map/ppermute | solution.py:105
  46.9 9.7 %collective-permute-done.3 = bf16[64,256]{1,0:T(8,128)(2,1)S(1)} collective-permute-done((bf16[64,256]{1,0:T(8,128)(2,1)S(1)}, bf16[64,256]{1,0:T(8,128)(2,1)S(1)}, u32[]{:S(2)}, u32[]{:S(2)}) %collective-permute-start.3) | collective-permute-done | bytes 32800 | tf_op jit(solution)/shard_map/ppermute | solution.py:105
  58.0 7.5 %collective-permute-done.21.refs_19_ = bf16[512,256]{1,0:T(8,128)(2,1)} collective-permute-done((bf16[512,256]{1,0:T(8,128)(2,1)}, bf16[512,256]{1,0:T(8,128)(2,1)}, u32[]{:S(2)}, u32[]{:S(2)}) %collective-permute-start.21) | collective-permute-done | bytes 262176 | tf_op jit(solution)/shard_map/ppermute | solution.py:94
  65.5 3.2 %collective-permute-start.25 = (bf16[512,256]{1,0:T(8,128)(2,1)}, bf16[512,256]{1,0:T(8,128)(2,1)S(1)}, u32[]{:S(2)}, u32[]{:S(2)}) collective-permute-start(bf16[512,256]{1,0:T(8,128)(2,1)} %collective-permute-done.17.refs_15_), channel_id=1, source_target_pairs={{0,16},{8,24},{16,32},{24,40},{32,48},{40,56},{48,0},{56,8},{64,80... | collective-permute-start | bytes 786440 | tf_op jit(solution)/shard_map/ppermute | solution.py:94
  68.7 2.7 %collective-permute-start.26 = (bf16[512,256]{1,0:T(8,128)(2,1)S(1)}, bf16[512,256]{1,0:T(8,128)(2,1)S(1)}, u32[]{:S(2)}, u32[]{:S(2)}) collective-permute-start(bf16[512,256]{1,0:T(8,128)(2,1)S(1)} %collective-permute-done.15.refs_13_), channel_id=1, source_target_pairs={{0,192},{8,200},{16,208},{24,216},{32,224},{40,232},{48,240},{56,2... | collective-permute-start | bytes 786440 | tf_op jit(solution)/shard_map/ppermute | solution.py:94
  76.3 6.8 %shard_map.82 = (bf16[16512,256]{1,0:T(8,128)(2,1)S(1)}, bf16[32,11,128,128]{3,2,1,0:T(8,128)(2,1)S(1)}) custom-call(s32[2]{0:T(128)S(1)} %pad_add_fusion.here_ref, bf16[8,32,256]{2,1,0:T(8,128)(2,1)S(1)} %bitcast.4, bf16[32,1,11,128,128]{4,3,2,1,0:T(8,128)(2,1)} %adj_hbm.1, bf16[512,256]{1,0:T(8,128)(2,1)S(1)} %multiply_convert_fusion.refs_0_, ...), custom_call_target="tpu_custom_call" | custom-call | flops 1703936000 | bytes 20971520 | tf_op jit(solution)/shard_map/pallas_call | solution.py:159
  83.2 6.5 %shard_map.83 = (bf16[2048,256]{1,0:T(8,128)(2,1)S(1)}, f32[2048,256]{1,0:T(8,128)S(1)}, bf16[16512,256]{1,0:T(8,128)(2,1)S(1)}, bf16[32,11,128,128]{3,2,1,0:T(8,128)(2,1)S(1)}) custom-call(s32[2]{0:T(128)S(1)} %pad_add_fusion.here_ref, s32[32,1,11]{2,1,0:T(1,128)S(1)} %copy.11.index_ref, ...), custom_call_target="tpu_custom_call", output_to_operand_aliasing={{2}: (4, {}), {3}: (5, {})} | custom-call | tf_op jit(solution)/shard_map/pallas_call | solution.py:224
  89.9 2.6 %collective-permute-done.27 = bf16[2048,256]{1,0:T(8,128)(2,1)S(1)} collective-permute-done((bf16[2048,256]{1,0:T(8,128)(2,1)S(1)}, bf16[2048,256]{1,0:T(8,128)(2,1)S(1)}, u32[]{:S(2)}, u32[]{:S(2)}) %collective-permute-start.27) | collective-permute-done | bytes 1048608 | tf_op jit(solution)/shard_map/ppermute | solution.py:244
  92.7 4.1 %collective-permute-start.28 = (bf16[256,256]{1,0:T(8,128)(2,1)S(1)}, bf16[256,256]{1,0:T(8,128)(2,1)S(1)}, u32[]{:S(2)}, u32[]{:S(2)}) collective-permute-start(bf16[256,256]{1,0:T(8,128)(2,1)S(1)} %get-tuple-element.59), channel_id=1, source_target_pairs={{0,6},{1,7},{2,0},{3,1},{4,2},{5,3},{6,4},{7,5},{8,14},{9,15},{10,... | collective-permute-start | bytes 393224 | tf_op jit(solution)/shard_map/ppermute | solution.py:255
  97.1 6.1 %collective-permute-done.29 = bf16[256,256]{1,0:T(8,128)(2,1)S(1)} collective-permute-done((bf16[256,256]{1,0:T(8,128)(2,1)S(1)}, bf16[256,256]{1,0:T(8,128)(2,1)S(1)}, u32[]{:S(2)}, u32[]{:S(2)}) %collective-permute-start.29) | collective-permute-done | bytes 131104 | tf_op jit(solution)/shard_map/ppermute | solution.py:252
  103.4 4.6 %collective-permute-done.32 = bf16[256,256]{1,0:T(8,128)(2,1)S(1)} collective-permute-done((bf16[256,256]{1,0:T(8,128)(2,1)S(1)}, bf16[256,256]{1,0:T(8,128)(2,1)S(1)}, u32[]{:S(2)}, u32[]{:S(2)}) %collective-permute-start.32) | collective-permute-done | bytes 131104 | tf_op jit(solution)/shard_map/ppermute | solution.py:255
  108.1 7.6 %collective-permute-done.30 = bf16[256,256]{1,0:T(8,128)(2,1)S(1)} collective-permute-done((bf16[256,256]{1,0:T(8,128)(2,1)S(1)}, bf16[256,256]{1,0:T(8,128)(2,1)S(1)}, u32[]{:S(2)}, u32[]{:S(2)}) %collective-permute-start.30) | collective-permute-done | bytes 131104 | tf_op jit(solution)/shard_map/ppermute | solution.py:252
  117.1 4.6 %collective-permute-done.33 = bf16[256,256]{1,0:T(8,128)(2,1)S(1)} collective-permute-done((bf16[256,256]{1,0:T(8,128)(2,1)S(1)}, bf16[256,256]{1,0:T(8,128)(2,1)S(1)}, u32[]{:S(2)}, u32[]{:S(2)}) %collective-permute-start.33) | collective-permute-done | bytes 131104 | tf_op jit(solution)/shard_map/ppermute | solution.py:255
  (90 shorter events, 26.5 us)
Async XLA Ops:
  1.8 8.1 %collective-permute-start.5 = (bf16[512,256]{1,0:T(8,128)(2,1)S(1)}, bf16[512,256]{1,0:T(8,128)(2,1)S(1)}, u32[]{:S(2)}, u32[]{:S(2)}) collective-permute-start(bf16[512,256]{1,0:T(8,128)(2,1)S(1)} %multiply_convert_fusion.refs_0_), channel_id=1, source_target_pairs={{0,16},{8,24},{16,32},{24,40},{32,48},{40,56},{48,0},{56,8},{64,80... | collective-permute-start | bytes 786440 | tf_op jit(solution)/shard_map/ppermute | solution.py:94
  4.1 7.6 %collective-permute-start.4 = (bf16[512,256]{1,0:T(8,128)(2,1)S(1)}, bf16[512,256]{1,0:T(8,128)(2,1)S(1)}, u32[]{:S(2)}, u32[]{:S(2)}) collective-permute-start(bf16[512,256]{1,0:T(8,128)(2,1)S(1)} %multiply_convert_fusion.refs_0_), channel_id=1, source_target_pairs={{0,48},{8,56},{16,0},{24,8},{32,16},{40,24},{48,32},{56,40},{64,11... | collective-permute-start | bytes 786440 | tf_op jit(solution)/shard_map/ppermute | solution.py:94
  4.1 8.6 %collective-permute-start.1 = (bf16[512,256]{1,0:T(8,128)(2,1)S(1)}, bf16[512,256]{1,0:T(8,128)(2,1)S(1)}, u32[]{:S(2)}, u32[]{:S(2)}) collective-permute-start(bf16[512,256]{1,0:T(8,128)(2,1)S(1)} %multiply_convert_fusion.refs_0_), channel_id=1, source_target_pairs={{0,64},{8,72},{16,80},{24,88},{32,96},{40,104},{48,112},{56,120},{... | collective-permute-start | bytes 786440 | tf_op jit(solution)/shard_map/ppermute | solution.py:94
  12.9 14.8 %collective-permute-start.11 = (bf16[1024,256]{1,0:T(8,128)(2,1)S(1)}, bf16[1024,256]{1,0:T(8,128)(2,1)S(1)}, u32[]{:S(2)}, u32[]{:S(2)}) collective-permute-start(bf16[1024,256]{1,0:T(8,128)(2,1)S(1)} %get-tuple-element.39), channel_id=1, source_target_pairs={{0,8},{8,0},{16,24},{24,16},{32,40},{40,32},{48,56},{56,48},{64,72... | collective-permute-start | bytes 1572872 | tf_op jit(solution)/shard_map/ppermute | solution.py:94
  18.9 7.7 %collective-permute-start.10 = (bf16[512,256]{1,0:T(8,128)(2,1)S(1)}, bf16[512,256]{1,0:T(8,128)(2,1)S(1)}, u32[]{:S(2)}, u32[]{:S(2)}) collective-permute-start(bf16[512,256]{1,0:T(8,128)(2,1)S(1)} %collective-permute-done.4.refs_2_), channel_id=1, source_target_pairs={{0,48},{8,56},{16,0},{24,8},{32,16},{40,24},{48,32},{56,40},{64,11... | collective-permute-start | bytes 786440 | tf_op jit(solution)/shard_map/ppermute | solution.py:94
  26.8 9.0 %collective-permute-start.14 = (bf16[512,256]{1,0:T(8,128)(2,1)S(1)}, bf16[512,256]{1,0:T(8,128)(2,1)S(1)}, u32[]{:S(2)}, u32[]{:S(2)}) collective-permute-start(bf16[512,256]{1,0:T(8,128)(2,1)S(1)} %collective-permute-done.2.refs_6_), channel_id=1, source_target_pairs={{0,48},{8,56},{16,0},{24,8},{32,16},{40,24},{48,32},{56,40},{64,11... | collective-permute-start | bytes 786440 | tf_op jit(solution)/shard_map/ppermute | solution.py:94
  27.7 12.2 %collective-permute-start.6 = (bf16[1024,256]{1,0:T(8,128)(2,1)S(1)}, bf16[1024,256]{1,0:T(8,128)(2,1)S(1)}, u32[]{:S(2)}, u32[]{:S(2)}) collective-permute-start(bf16[1024,256]{1,0:T(8,128)(2,1)S(1)} %get-tuple-element.36), channel_id=1, source_target_pairs={{0,64},{8,72},{16,80},{24,88},{32,96},{40,104},{48,112},{56,120},{... | collective-permute-start | bytes 1572872 | tf_op jit(solution)/shard_map/ppermute | solution.py:94
  31.5 33.9 %collective-permute-start.16 = (bf16[1536,256]{1,0:T(8,128)(2,1)}, bf16[1536,256]{1,0:T(8,128)(2,1)}, u32[]{:S(2)}, u32[]{:S(2)}) collective-permute-start(bf16[1536,256]{1,0:T(8,128)(2,1)} %get-tuple-element.44), channel_id=1, source_target_pairs={{0,192},{8,200},{16,208},{24,216},{32,224},{40,232},{48,240},{56,2... | collective-permute-start | bytes 2359304 | tf_op jit(solution)/shard_map/ppermute | solution.py:94
  35.8 7.7 %collective-permute-start.18 = (bf16[512,256]{1,0:T(8,128)(2,1)S(1)}, bf16[512,256]{1,0:T(8,128)(2,1)S(1)}, u32[]{:S(2)}, u32[]{:S(2)}) collective-permute-start(bf16[512,256]{1,0:T(8,128)(2,1)S(1)} %collective-permute-done.14.refs_12_), channel_id=1, source_target_pairs={{0,48},{8,56},{16,0},{24,8},{32,16},{40,24},{48,32},{56,40},{64,11... | collective-permute-start | bytes 786440 | tf_op jit(solution)/shard_map/ppermute | solution.py:94
  36.7 28.7 %collective-permute-start.19 = (bf16[1024,256]{1,0:T(8,128)(2,1)}, bf16[1024,256]{1,0:T(8,128)(2,1)}, u32[]{:S(2)}, u32[]{:S(2)}) collective-permute-start(bf16[1024,256]{1,0:T(8,128)(2,1)} %pad_maximum_fusion.4), channel_id=1, source_target_pairs={{0,16},{8,24},{16,32},{24,40},{32,48},{40,56},{48,0},{56,8},{64,80... | collective-permute-start | bytes 1572872 | tf_op jit(solution)/shard_map/ppermute | solution.py:94
  40.7 42.5 %collective-permute-start.22 = (bf16[1536,256]{1,0:T(8,128)(2,1)}, bf16[1536,256]{1,0:T(8,128)(2,1)S(1)}, u32[]{:S(2)}, u32[]{:S(2)}) collective-permute-start(bf16[1536,256]{1,0:T(8,128)(2,1)} %get-tuple-element.52), channel_id=1, source_target_pairs={{0,64},{8,72},{16,80},{24,88},{32,96},{40,104},{48,112},{56,120},{... | collective-permute-start | bytes 2359304 | tf_op jit(solution)/shard_map/ppermute | solution.py:94
  42.3 14.7 %collective-permute-start.20 = (bf16[512,256]{1,0:T(8,128)(2,1)}, bf16[512,256]{1,0:T(8,128)(2,1)}, u32[]{:S(2)}, u32[]{:S(2)}) collective-permute-start(bf16[512,256]{1,0:T(8,128)(2,1)} %collective-permute-done.9.refs_5_), channel_id=1, source_target_pairs={{0,8},{8,0},{16,24},{24,16},{32,40},{40,32},{48,56},{56,48},{64,72... | collective-permute-start | bytes 786440 | tf_op jit(solution)/shard_map/ppermute | solution.py:94
  44.2 12.5 %collective-permute-start.3 = (bf16[64,256]{1,0:T(8,128)(2,1)S(1)}, bf16[64,256]{1,0:T(8,128)(2,1)S(1)}, u32[]{:S(2)}, u32[]{:S(2)}) collective-permute-start(bf16[64,256]{1,0:T(8,128)(2,1)S(1)} %pad_maximum_fusion.7), channel_id=1, source_target_pairs={{0,2},{1,3},{2,4},{3,5},{4,6},{5,7},{6,0},{7,1},{8,10},{9,11},{10,... | collective-permute-start | bytes 98312 | tf_op jit(solution)/shard_map/ppermute | solution.py:105
  56.7 8.8 %collective-permute-start.21 = (bf16[512,256]{1,0:T(8,128)(2,1)}, bf16[512,256]{1,0:T(8,128)(2,1)}, u32[]{:S(2)}, u32[]{:S(2)}) collective-permute-start(bf16[512,256]{1,0:T(8,128)(2,1)} %collective-permute-done.17.refs_15_), channel_id=1, source_target_pairs={{0,48},{8,56},{16,0},{24,8},{32,16},{40,24},{48,32},{56,40},{64,11... | collective-permute-start | bytes 786440 | tf_op jit(solution)/shard_map/ppermute | solution.py:94
  57.0 11.7 %collective-permute-start.7 = (bf16[128,256]{1,0:T(8,128)(2,1)S(1)}, bf16[128,256]{1,0:T(8,128)(2,1)S(1)}, u32[]{:S(2)}, u32[]{:S(2)}) collective-permute-start(bf16[128,256]{1,0:T(8,128)(2,1)S(1)} %pad_maximum_fusion.6), channel_id=1, source_target_pairs={{0,4},{1,5},{2,6},{3,7},{4,0},{5,1},{6,2},{7,3},{8,12},{9,13},{10,... | collective-permute-start | bytes 196616 | tf_op jit(solution)/shard_map/ppermute | solution.py:107
  65.4 17.7 %collective-permute-start.23 = (bf16[512,256]{1,0:T(8,128)(2,1)}, bf16[512,256]{1,0:T(8,128)(2,1)S(1)}, u32[]{:S(2)}, u32[]{:S(2)}) collective-permute-start(bf16[512,256]{1,0:T(8,128)(2,1)} %copy-done.4), channel_id=1, source_target_pairs={{0,8},{8,0},{16,24},{24,16},{32,40},{40,32},{48,56},{56,48},{64,72... | collective-permute-start | bytes 786440 | tf_op jit(solution)/shard_map/ppermute | solution.py:94
  65.4 17.7 %collective-permute-start.24 = (bf16[512,256]{1,0:T(8,128)(2,1)}, bf16[512,256]{1,0:T(8,128)(2,1)S(1)}, u32[]{:S(2)}, u32[]{:S(2)}) collective-permute-start(bf16[512,256]{1,0:T(8,128)(2,1)} %collective-permute-done.21.refs_19_), channel_id=1, source_target_pairs={{0,48},{8,56},{16,0},{24,8},{32,16},{40,24},{48,32},{56,40},{64,11... | collective-permute-start | bytes 786440 | tf_op jit(solution)/shard_map/ppermute | solution.py:94
  65.5 17.7 %collective-permute-start.25 = (bf16[512,256]{1,0:T(8,128)(2,1)}, bf16[512,256]{1,0:T(8,128)(2,1)S(1)}, u32[]{:S(2)}, u32[]{:S(2)}) collective-permute-start(bf16[512,256]{1,0:T(8,128)(2,1)} %collective-permute-done.17.refs_15_), channel_id=1, source_target_pairs={{0,16},{8,24},{16,32},{24,40},{32,48},{40,56},{48,0},{56,8},{64,80... | collective-permute-start | bytes 786440 | tf_op jit(solution)/shard_map/ppermute | solution.py:94
  68.7 14.5 %collective-permute-start.26 = (bf16[512,256]{1,0:T(8,128)(2,1)S(1)}, bf16[512,256]{1,0:T(8,128)(2,1)S(1)}, u32[]{:S(2)}, u32[]{:S(2)}) collective-permute-start(bf16[512,256]{1,0:T(8,128)(2,1)S(1)} %collective-permute-done.15.refs_13_), channel_id=1, source_target_pairs={{0,192},{8,200},{16,208},{24,216},{32,224},{40,232},{48,240},{56,2... | collective-permute-start | bytes 786440 | tf_op jit(solution)/shard_map/ppermute | solution.py:94
  92.6 10.6 %collective-permute-start.29 = (bf16[256,256]{1,0:T(8,128)(2,1)S(1)}, bf16[256,256]{1,0:T(8,128)(2,1)S(1)}, u32[]{:S(2)}, u32[]{:S(2)}) collective-permute-start(bf16[256,256]{1,0:T(8,128)(2,1)S(1)} %get-tuple-element.60), channel_id=1, source_target_pairs={{0,2},{1,3},{2,4},{3,5},{4,6},{5,7},{6,0},{7,1},{8,10},{9,11},{10,... | collective-permute-start | bytes 393224 | tf_op jit(solution)/shard_map/ppermute | solution.py:252
  92.7 10.7 %collective-permute-start.28 = (bf16[256,256]{1,0:T(8,128)(2,1)S(1)}, bf16[256,256]{1,0:T(8,128)(2,1)S(1)}, u32[]{:S(2)}, u32[]{:S(2)}) collective-permute-start(bf16[256,256]{1,0:T(8,128)(2,1)S(1)} %get-tuple-element.59), channel_id=1, source_target_pairs={{0,6},{1,7},{2,0},{3,1},{4,2},{5,3},{6,4},{7,5},{8,14},{9,15},{10,... | collective-permute-start | bytes 393224 | tf_op jit(solution)/shard_map/ppermute | solution.py:255
  96.9 11.2 %collective-permute-start.32 = (bf16[256,256]{1,0:T(8,128)(2,1)S(1)}, bf16[256,256]{1,0:T(8,128)(2,1)S(1)}, u32[]{:S(2)}, u32[]{:S(2)}) collective-permute-start(bf16[256,256]{1,0:T(8,128)(2,1)S(1)} %get-tuple-element.62), channel_id=1, source_target_pairs={{0,6},{1,7},{2,0},{3,1},{4,2},{5,3},{6,4},{7,5},{8,14},{9,15},{10,... | collective-permute-start | bytes 393224 | tf_op jit(solution)/shard_map/ppermute | solution.py:255
  103.2 12.5 %collective-permute-start.30 = (bf16[256,256]{1,0:T(8,128)(2,1)S(1)}, bf16[256,256]{1,0:T(8,128)(2,1)S(1)}, u32[]{:S(2)}, u32[]{:S(2)}) collective-permute-start(bf16[256,256]{1,0:T(8,128)(2,1)S(1)} %add_convert_fusion.1), channel_id=1, source_target_pairs={{0,2},{1,3},{2,4},{3,5},{4,6},{5,7},{6,0},{7,1},{8,10},{9,11},{10,... | collective-permute-start | bytes 393224 | tf_op jit(solution)/shard_map/ppermute | solution.py:252
  103.3 13.8 %collective-permute-start.31 = (bf16[256,256]{1,0:T(8,128)(2,1)S(1)}, bf16[256,256]{1,0:T(8,128)(2,1)S(1)}, u32[]{:S(2)}, u32[]{:S(2)}) collective-permute-start(bf16[256,256]{1,0:T(8,128)(2,1)S(1)} %get-tuple-element.61), channel_id=1, source_target_pairs={{0,2},{1,3},{2,4},{3,5},{4,6},{5,7},{6,0},{7,1},{8,10},{9,11},{10,... | collective-permute-start | bytes 393224 | tf_op jit(solution)/shard_map/ppermute | solution.py:252
  (24 other events, 181.4 us)

commit v2 on v1

v2 whole, which is shorter than its diff:
```python
import functools

import jax
import jax.numpy as jnp
from jax import lax
from jax.experimental import pallas as pl
from jax.experimental.pallas import tpu as pltpu
from jax.sharding import PartitionSpec as P

NX, NY, NZ = 4, 4, 2
NH = 4
PANEL = 512
BLOCK = 128
F = 256
RB = 32
MAXB = 11
KPER = PANEL // BLOCK
SHARDS = NX * NY * NZ
ADJ_COPIES = 4
KERNEL_VMEM = 20 << 20
HIDDEN = pltpu.VMEM((SHARDS * PANEL + BLOCK, F), jnp.bfloat16)
ADJ = pltpu.VMEM((RB, MAXB, BLOCK, BLOCK), jnp.bfloat16)

PLAN = (
    (0, -1, ((0, 0, 0),)),
    (1, 1, ((0, 0, 0),)),
    (1, -1, ((0, 0, 0),)),
    (0, 1, ((0, 0, 0),)),
    (0, -1, ((3, 0, 0),)),
    (1, 1, ((3, 0, 0),)),
    (1, -1, ((0, 3, 0),)),
    (0, 1, ((0, 3, 0),)),
    (2, 1, ((0, 1, 0),)),
    (0, -1, ((0, 3, 0),)),
    (1, 1, ((1, 0, 0),)),
    (1, -1, ((2, 0, 0),)),
    (0, 1, ((0, 2, 0),)),
    (2, 1, ((0, 3, 0),)),
    (0, -1, ((0, 2, 0),)),
    (1, 1, ((2, 0, 0),)),
    (1, -1, ((2, 3, 0),)),
    (0, 1, ((0, 1, 1),)),
    (2, 1, ((2, 3, 0),)),
    (0, -1, ((0, 1, 1),)),
    (1, 1, ((0, 1, 1),)),
    (1, -1, ((0, 1, 1),)),
    (0, 1, ((0, 3, 1),)),
    (2, 1, ((1, 0, 0),)),
    (0, -1, ((3, 1, 1),)),
    (1, 1, ((2, 3, 1),)),
    (0, 1, ((0, 2, 1),)),
    (2, 1, ((3, 3, 0),)),
    (1, -1, ((3, 1, 1),)),
    (0, -1, ((0, 2, 1),)),
    (1, 1, ((2, 1, 1),)),
)
LATE = (26, 27, 28, 29, 30)


def row_perm(axis, step):
    pairs = []
    for y in range(NY):
        for x in range(NX):
            for z in range(NZ):
                c = [x, y, z]
                c[axis] = (c[axis] + step) % (NX, NY, NZ)[axis]
                pairs.append(((y * NX + x) * NZ + z, (c[1] * NX + c[0]) * NZ + c[2]))
    return pairs


def col_perm(dz, core):
    return [(h * 2 + c, ((h + dz) % NH) * 2 + (c ^ core)) for h in range(NH) for c in range(2)]


def after(value, *others):
    return lax.optimization_barrier((value, *others))[0]


def moved(place, axis, step):
    place = list(place)
    place[axis] = (place[axis] + step) % (NX, NY, NZ)[axis]
    return tuple(place)


def gather_rows(mine, before_z):
    arrays, at, last = [(mine, ((0, 0, 0),))], {(0, 0, 0): (0, 0)}, {}
    for axis, step, sources in PLAN:
        index = at[sources[0]][0]
        if arrays[index][1] == sources:
            value = arrays[index][0]
        else:
            rows = []
            for source in sources:
                index, n = at[source]
                array = arrays[index][0]
                rows.append(array if len(arrays[index][1]) == 1 else array[n * PANEL : (n + 1) * PANEL])
            value = rows[0] if len(rows) == 1 else jnp.concatenate(rows)
        link = (axis, step)
        if link in last:
            value = after(value, last[link])
        elif axis == 2:
            value = after(value, before_z)
        last[link] = got = lax.ppermute(value, "row", row_perm(axis, step))
        places = tuple(moved(source, axis, step) for source in sources)
        for n, place in enumerate(places):
            at[place] = (len(arrays), n)
        arrays.append((got, places))
    return arrays


def gather_weight(weight):
    pair = jnp.concatenate([weight, lax.ppermute(weight, "col", col_perm(0, 1))])
    quad = jnp.concatenate([pair, lax.ppermute(pair, "col", col_perm(1, 0))])
    whole = jnp.concatenate([quad, lax.ppermute(quad, "col", col_perm(2, 0))])
    return whole.reshape(NH * 2, F // (NH * 2), F)


def lay_weight(here_ref, weight_ref, weight):
    col = here_ref[1]
    rows = F // (NH * 2)
    for n in range(NH * 2):
        place = ((lax.shift_right_logical(col, 1) - n // 2) & (NH - 1)) * 2 + ((col & 1) ^ (n % 2))
        weight[pl.ds(pl.multiple_of(place * rows, rows), rows), :] = weight_ref[n]


def hidden_rows(pieces, weight, hidden, at):
    for piece in pieces:
        rows = pl.ds(at, piece.shape[0])
        hidden[rows, :] = jnp.dot(piece[...], weight[...], preferred_element_type=jnp.float32).astype(jnp.bfloat16)
        at += piece.shape[0]


def early_kernel(here_ref, weight_ref, adj_hbm, *refs):
    *pieces, hidden, adj, weight, sems = refs
    part = RB // ADJ_COPIES
    copies = [
        pltpu.make_async_copy(adj_hbm.at[pl.ds(n * part, part), 0], adj.at[pl.ds(n * part, part)], sems.at[n])
        for n in range(ADJ_COPIES)
    ]
    for copy in copies:
        copy.start()
    lay_weight(here_ref, weight_ref, weight)
    hidden[pl.ds(SHARDS * PANEL, BLOCK), :] = jnp.zeros((BLOCK, F), jnp.bfloat16)
    hidden_rows(pieces, weight, hidden, 0)
    for copy in copies:
        copy.wait()


def early(here, weight_rows, adjacency, pieces):
    smem, vmem, anywhere = (pl.BlockSpec(memory_space=m) for m in (pltpu.SMEM, pltpu.VMEM, pl.ANY))
    return pl.pallas_call(
        early_kernel,
        in_specs=[smem, vmem, anywhere] + [vmem] * len(pieces),
        out_specs=[vmem, vmem],
        scratch_shapes=[pltpu.VMEM((F, F), jnp.bfloat16), pltpu.SemaphoreType.DMA((ADJ_COPIES,))],
        out_shape=[HIDDEN, ADJ],
        compiler_params=pltpu.CompilerParams(vmem_limit_bytes=KERNEL_VMEM),
        cost_estimate=pl.CostEstimate(flops=2 * 13000 * F * F, bytes_accessed=20 << 20, transcendentals=0),
    )(here, weight_rows, adjacency, *pieces)


def products(here_ref, index_ref, count_ref, hidden, adj, table, order, side, out_ref):
    row, col = here_ref[0], here_ref[1]
    y, x, z = lax.shift_right_logical(row, 3), lax.shift_right_logical(row, 1) & (NX - 1), row & (NZ - 1)
    chip, core = lax.shift_right_logical(col, 1), (col & 1) ^ side
    for n, (dx, dy, dz) in enumerate(order):
        shard = (((y - dy) & (NY - 1)) * NX + ((x - dx) & (NX - 1))) * NZ + (z ^ dz)
        table[shard] = n * PANEL

    def rows_at(block, m):
        column = index_ref[block, 0, m]
        start = table[lax.shift_right_logical(column, 2)] + (column & (KPER - 1)) * BLOCK
        start = jnp.where(m < count_ref[block, 0], start, SHARDS * PANEL)
        return hidden[pl.ds(pl.multiple_of(start, BLOCK), BLOCK), :]

    def total_of(block):
        right = [rows_at(block, m) for m in range(MAXB)]
        left = [adj[block, m] for m in range(MAXB)]
        return jnp.dot(
            jnp.concatenate(left, axis=1), jnp.concatenate(right, axis=0), preferred_element_type=jnp.float32
        )

    def body(d, _):
        panel = ((chip + d) & (NH - 1)) * 2 + core
        for j in range(KPER):
            at = pl.ds(pl.multiple_of(d * PANEL + j * BLOCK, BLOCK), BLOCK)
            out_ref[at, :] = total_of(panel * KPER + j).astype(out_ref.dtype)
        return 0

    lax.fori_loop(0, NH, body, 0)


def send_kernel(order, here_ref, index_ref, count_ref, hidden_in, adj_in, weight_ref, *refs):
    *pieces, send_ref, hidden, adj, weight, table = refs
    del hidden_in, adj_in
    lay_weight(here_ref, weight_ref, weight)
    hidden_rows(pieces, weight, hidden, SHARDS * PANEL - sum(piece.shape[0] for piece in pieces))
    products(here_ref, index_ref, count_ref, hidden, adj, table, order, 1, send_ref)


def keep_kernel(order, here_ref, index_ref, count_ref, hidden_in, adj_in, keep_ref, hidden, adj, table):
    del hidden_in, adj_in
    products(here_ref, index_ref, count_ref, hidden, adj, table, order, 0, keep_ref)


def aggregate(kernel, order, dtype, here, index, counts, hidden, adj, *more):
    smem, vmem = (pl.BlockSpec(memory_space=m) for m in (pltpu.SMEM, pltpu.VMEM))
    weight = [pltpu.VMEM((F, F), jnp.bfloat16)] if more else []
    return pl.pallas_call(
        functools.partial(kernel, order),
        in_specs=[smem, smem, smem, vmem, vmem] + [vmem] * len(more),
        out_specs=[vmem, vmem, vmem],
        scratch_shapes=weight + [pltpu.SMEM((SHARDS,), jnp.int32)],
        out_shape=[pltpu.VMEM((NH * PANEL, F), dtype), HIDDEN, ADJ],
        input_output_aliases={3: 1, 4: 2},
        compiler_params=pltpu.CompilerParams(vmem_limit_bytes=KERNEL_VMEM),
        cost_estimate=pl.CostEstimate(flops=1500000000, bytes_accessed=8 << 20, transcendentals=0),
    )(here, index, counts, hidden, adj, *more)


def reduce_chips(got, keep):
    h = PANEL // 2

    def part(d, side):
        at = d * PANEL + side * h
        return keep[at : at + h] + got[at : at + h].astype(jnp.float32)

    def plus(value):
        return lax.ppermute(value.astype(jnp.bfloat16), "col", col_perm(1, 0)).astype(jnp.float32)

    def minus(value):
        return lax.ppermute(value.astype(jnp.bfloat16), "col", col_perm(-1, 0)).astype(jnp.float32)

    first = [part(2, 0), part(2, 1), part(1, 1), part(3, 0)]
    first = lax.optimization_barrier([value.astype(jnp.bfloat16) for value in first])
    far_top, far_bottom = plus(first[0]), minus(first[1])
    near_bottom, near_top = plus(first[2]), minus(first[3])
    chain_top = plus(part(1, 0) + far_top)
    chain_bottom = minus(part(3, 1) + far_bottom)
    top = part(0, 0) + near_top + chain_top
    bottom = part(0, 1) + near_bottom + chain_bottom
    return jnp.concatenate([top, bottom])


def on_device(
    feature_codes,
    bit_widths,
    row_scales,
    weight,
    layer_bias,
    adjacency_blocks,
    block_index,
    block_counts,
):
    here = jnp.stack([lax.axis_index("row"), lax.axis_index("col")]).astype(jnp.int32)
    shift = 8 - bit_widths[0]
    level = jnp.left_shift(jnp.right_shift(feature_codes, shift), shift)
    features = (level.astype(jnp.float32) * row_scales[:, None]).astype(jnp.bfloat16)
    weight_rows = gather_weight(weight)
    arrays = gather_rows(features, weight_rows)

    soon = [a for n, a in enumerate(arrays) if n - 1 not in LATE]
    last = [arrays[n + 1] for n in LATE]
    order = [place for _, places in soon + last for place in places]
    blocks = pltpu.with_memory_space_constraint(adjacency_blocks, pltpu.HBM)
    hidden, adj = early(here, weight_rows, blocks, [a for a, _ in soon])
    tables = (here, block_index, block_counts)
    send, hidden, adj = aggregate(
        send_kernel, order, jnp.bfloat16, *tables, hidden, adj, weight_rows, *[a for a, _ in last]
    )
    got = lax.ppermute(send, "col", col_perm(0, 1))
    keep, _, _ = aggregate(keep_kernel, order, jnp.float32, *tables, hidden, adj)
    summed = reduce_chips(got, keep)
    return jnp.maximum(summed + layer_bias[None, :], 0.0).astype(jnp.bfloat16)


def solution(mesh):
    in_specs = (
        P(("row", "col"), None),
        P(("row", "col")),
        P(("row", "col")),
        P("col", None),
        P(),
        P("row", "col", None, None, None),
        P("row", "col", None),
        P("row", "col"),
    )
    out_specs = P(("row", "col"), None)
    return jax.shard_map(
        on_device, mesh=mesh, in_specs=in_specs, out_specs=out_specs, check_vma=False
    )
```

time: 123 us -> 126 us (1.024)
  the two profiles are of different devices: /device:TPU:6 before, /device:TPU:26 now
where the time goes in v2:
time: 126 us
  starting transfers between devices  72.8 us (58%)
  waiting for transfers between devices  21.8 us (17%)
  Pallas kernels  13.5 us (11%)
  local copies, waits for them, and re-layouts  12.1 us (10%)
  other arithmetic  4.52 us (4%)
    ppermute x31, starting transfers between devices, gather_rows(): last[link] = got = lax.ppermute(value, 'row', row_perm(axis, step))  48.2 us
    unnamed x30, local copies, waits for them, and re-layouts  12.1 us
    ppermute x3, starting transfers between devices, plus(): lax.ppermute(value.astype(jnp.bfloat16), 'col', col_perm(1, 0))  10.6 us
    ppermute x3, waiting for transfers between devices, minus(): lax.ppermute(value.astype(jnp.bfloat16), 'col', col_perm(-1, 0))  8.69 us
    pallas_call x2, Pallas kernels, aggregate(): pl.pallas_call(functools.partial(kernel, order), in_specs=[smem, smem, sm...  7.54 us
    ppermute x3, starting transfers between devices, minus(): lax.ppermute(value.astype(jnp.bfloat16), 'col', col_perm(-1, 0))  6.91 us
    pallas_call x1, Pallas kernels, early(): pl.pallas_call(early_kernel, in_specs=[smem, vmem, anywhere] + [vmem] * l...  5.94 us
    ppermute x1, starting transfers between devices, gather_weight(): whole = jnp.concatenate([quad, lax.ppermute(quad, 'col', col_perm(2, 0))])  5.42 us
  transfers between devices with their start and end apart: 41, of which 11 were waited for; matrix products, arithmetic and copies ran while one was open for 4% of the time, Pallas kernels for 8%

profile of v2, /device:TPU:26, one launch (start us, length us, event | category | flops | bytes accessed | tf_op | source)
XLA Modules:
  0.0 125.5 jit_solution(1238438629200703138)
XLA Ops:
  2.1 2.3 %collective-permute-start.3 = (bf16[512,256]{1,0:T(8,128)(2,1)S(1)}, bf16[512,256]{1,0:T(8,128)(2,1)S(1)}, u32[]{:S(2)}, u32[]{:S(2)}) collective-permute-start(bf16[512,256]{1,0:T(8,128)(2,1)S(1)} %multiply_convert_fusion.refs_0_), channel_id=1, source_target_pairs={{0,48},{8,56},{16,0},{24,8},{32,16},{40,24},{48,32},{56,40},{64,11... | collective-permute-start | bytes 786440 | tf_op jit(solution)/shard_map/ppermute | solution.py:103
  14.8 5.4 %collective-permute-start.2 = (bf16[128,256]{1,0:T(8,128)(2,1)S(1)}, bf16[128,256]{1,0:T(8,128)(2,1)S(1)}, u32[]{:S(2)}, u32[]{:S(2)}) collective-permute-start(bf16[128,256]{1,0:T(8,128)(2,1)S(1)} %pad_maximum_fusion.1), channel_id=1, source_target_pairs={{0,4},{1,5},{2,6},{3,7},{4,0},{5,1},{6,2},{7,3},{8,12},{9,13},{10,... | collective-permute-start | bytes 196616 | tf_op jit(solution)/shard_map/ppermute | solution.py:114
  20.2 2.8 %collective-permute-done.2 = bf16[128,256]{1,0:T(8,128)(2,1)S(1)} collective-permute-done((bf16[128,256]{1,0:T(8,128)(2,1)S(1)}, bf16[128,256]{1,0:T(8,128)(2,1)S(1)}, u32[]{:S(2)}, u32[]{:S(2)}) %collective-permute-start.2) | collective-permute-done | bytes 65568 | tf_op jit(solution)/shard_map/ppermute | solution.py:114
  29.6 2.6 %collective-permute-start.13 = (bf16[512,256]{1,0:T(8,128)(2,1)S(1)}, bf16[512,256]{1,0:T(8,128)(2,1)S(1)}, u32[]{:S(2)}, u32[]{:S(2)}) collective-permute-start(bf16[512,256]{1,0:T(8,128)(2,1)S(1)} %collective-permute-done.6.refs_4_), channel_id=1, source_target_pairs={{0,64},{8,72},{16,80},{24,88},{32,96},{40,104},{48,112},{56,120},{... | collective-permute-start | bytes 786440 | tf_op jit(solution)/shard_map/ppermute | solution.py:103
  33.9 2.3 %collective-permute-start.15 = (bf16[512,256]{1,0:T(8,128)(2,1)S(1)}, bf16[512,256]{1,0:T(8,128)(2,1)S(1)}, u32[]{:S(2)}, u32[]{:S(2)}) collective-permute-start(bf16[512,256]{1,0:T(8,128)(2,1)S(1)} %collective-permute-done.9.refs_7_), channel_id=1, source_target_pairs={{0,16},{8,24},{16,32},{24,40},{32,48},{40,56},{48,0},{56,8},{64,80... | collective-permute-start | bytes 786440 | tf_op jit(solution)/shard_map/ppermute | solution.py:103
  37.1 3.1 %collective-permute-start.18 = (bf16[512,256]{1,0:T(8,128)(2,1)S(1)}, bf16[512,256]{1,0:T(8,128)(2,1)S(1)}, u32[]{:S(2)}, u32[]{:S(2)}) collective-permute-start(bf16[512,256]{1,0:T(8,128)(2,1)S(1)} %collective-permute-done.7.refs_5_), channel_id=1, source_target_pairs={{0,64},{8,72},{16,80},{24,88},{32,96},{40,104},{48,112},{56,120},{... | collective-permute-start | bytes 786440 | tf_op jit(solution)/shard_map/ppermute | solution.py:103
  42.5 3.4 %collective-permute-start.20 = (bf16[512,256]{1,0:T(8,128)(2,1)S(1)}, bf16[512,256]{1,0:T(8,128)(2,1)S(1)}, u32[]{:S(2)}, u32[]{:S(2)}) collective-permute-start(bf16[512,256]{1,0:T(8,128)(2,1)S(1)} %collective-permute-done.11.refs_9_), channel_id=1, source_target_pairs={{0,16},{8,24},{16,32},{24,40},{32,48},{40,56},{48,0},{56,8},{64,80... | collective-permute-start | bytes 786440 | tf_op jit(solution)/shard_map/ppermute | solution.py:103
  47.3 2.9 %collective-permute-start.23 = (bf16[512,256]{1,0:T(8,128)(2,1)S(1)}, bf16[512,256]{1,0:T(8,128)(2,1)S(1)}, u32[]{:S(2)}, u32[]{:S(2)}) collective-permute-start(bf16[512,256]{1,0:T(8,128)(2,1)S(1)} %collective-permute-done.11.refs_9_), channel_id=1, source_target_pairs={{0,64},{8,72},{16,80},{24,88},{32,96},{40,104},{48,112},{56,120},{... | collective-permute-start | bytes 786440 | tf_op jit(solution)/shard_map/ppermute | solution.py:103
  52.8 2.5 %collective-permute-start.25 = (bf16[512,256]{1,0:T(8,128)(2,1)}, bf16[512,256]{1,0:T(8,128)(2,1)}, u32[]{:S(2)}, u32[]{:S(2)}) collective-permute-start(bf16[512,256]{1,0:T(8,128)(2,1)} %collective-permute-done.16.refs_14_), channel_id=1, source_target_pairs={{0,16},{8,24},{16,32},{24,40},{32,48},{40,56},{48,0},{56,8},{64,80... | collective-permute-start | bytes 786440 | tf_op jit(solution)/shard_map/ppermute | solution.py:103
  56.5 3.5 %collective-permute-start.28 = (bf16[512,256]{1,0:T(8,128)(2,1)}, bf16[512,256]{1,0:T(8,128)(2,1)}, u32[]{:S(2)}, u32[]{:S(2)}) collective-permute-start(bf16[512,256]{1,0:T(8,128)(2,1)} %collective-permute-done.21.refs_19_), channel_id=1, source_target_pairs={{0,64},{8,72},{16,80},{24,88},{32,96},{40,104},{48,112},{56,120},{... | collective-permute-start | bytes 786440 | tf_op jit(solution)/shard_map/ppermute | solution.py:103
  64.3 2.3 %collective-permute-done.28.refs_26_ = bf16[512,256]{1,0:T(8,128)(2,1)} collective-permute-done((bf16[512,256]{1,0:T(8,128)(2,1)}, bf16[512,256]{1,0:T(8,128)(2,1)}, u32[]{:S(2)}, u32[]{:S(2)}) %collective-permute-start.28) | collective-permute-done | bytes 262176 | tf_op jit(solution)/shard_map/ppermute | solution.py:103
  66.6 3.7 %collective-permute-start.33 = (bf16[512,256]{1,0:T(8,128)(2,1)}, bf16[512,256]{1,0:T(8,128)(2,1)S(1)}, u32[]{:S(2)}, u32[]{:S(2)}) collective-permute-start(bf16[512,256]{1,0:T(8,128)(2,1)} %collective-permute-done.27.refs_25_), channel_id=1, source_target_pairs={{0,64},{8,72},{16,80},{24,88},{32,96},{40,104},{48,112},{56,120},{... | collective-permute-start | bytes 786440 | tf_op jit(solution)/shard_map/ppermute | solution.py:103
  70.3 3.2 %collective-permute-start.32 = (bf16[512,256]{1,0:T(8,128)(2,1)}, bf16[512,256]{1,0:T(8,128)(2,1)S(1)}, u32[]{:S(2)}, u32[]{:S(2)}) collective-permute-start(bf16[512,256]{1,0:T(8,128)(2,1)} %copy-done.8), channel_id=1, source_target_pairs={{0,48},{8,56},{16,0},{24,8},{32,16},{40,24},{48,32},{56,40},{64,11... | collective-permute-start | bytes 786440 | tf_op jit(solution)/shard_map/ppermute | solution.py:103
  79.3 5.9 %shard_map.82 = (bf16[16512,256]{1,0:T(8,128)(2,1)S(1)}, bf16[32,11,128,128]{3,2,1,0:T(8,128)(2,1)S(1)}) custom-call(s32[2]{0:T(128)S(1)} %pad_add_fusion.here_ref, bf16[8,32,256]{2,1,0:T(8,128)(2,1)S(1)} %bitcast.4, bf16[32,1,11,128,128]{4,3,2,1,0:T(8,128)(2,1)} %adj_hbm.1, bf16[512,256]{1,0:T(8,128)(2,1)S(1)} %multiply_convert_fusion.refs_0_, ...), custom_call_target="tpu_custom_call" | custom-call | flops 1703936000 | bytes 20971520 | tf_op jit(solution)/shard_map/pallas_call | solution.py:151
  85.3 4.0 %shard_map.83 = (bf16[2048,256]{1,0:T(8,128)(2,1)S(1)}, bf16[16512,256]{1,0:T(8,128)(2,1)S(1)}, bf16[32,11,128,128]{3,2,1,0:T(8,128)(2,1)S(1)}) custom-call(s32[2]{0:T(128)S(1)} %pad_add_fusion.here_ref, s32[32,1,11]{2,1,0:T(1,128)S(1)} %copy.15.index_ref, s32[32,1]{1,0:T(8,128)S(1)} %copy-done.12, ...), custom_call_target="tpu_custom_call", output_to_operand_aliasing={{1}: (3, {}), {2}: (4, {})} | custom-call | flops 1500000000 | bytes 8388608 | tf_op jit(solution)/shard_map/pallas_call | solution.py:209
  89.4 3.6 %shard_map.84 = (f32[2048,256]{1,0:T(8,128)S(1)}, bf16[16512,256]{1,0:T(8,128)(2,1)S(1)}, bf16[32,11,128,128]{3,2,1,0:T(8,128)(2,1)S(1)}) custom-call(s32[2]{0:T(128)S(1)} %pad_add_fusion.here_ref, s32[32,1,11]{2,1,0:T(1,128)S(1)} %copy.15.index_ref, s32[32,1]{1,0:T(8,128)S(1)} %copy-done.12, ...), custom_call_target="tpu_custom_call", output_to_operand_aliasing={{1}: (3, {}), {2}: (4, {})} | custom-call | flops 1500000000 | bytes 8388608 | tf_op jit(solution)/shard_map/pallas_call | solution.py:209
  93.1 3.1 %collective-permute-start.36 = (bf16[256,256]{1,0:T(8,128)(2,1)S(1)}, bf16[256,256]{1,0:T(8,128)(2,1)S(1)}, u32[]{:S(2)}, u32[]{:S(2)}) collective-permute-start(bf16[256,256]{1,0:T(8,128)(2,1)S(1)} %get-tuple-element.76), channel_id=1, source_target_pairs={{0,2},{1,3},{2,4},{3,5},{4,6},{5,7},{6,0},{7,1},{8,10},{9,11},{10,... | collective-permute-start | bytes 393224 | tf_op jit(solution)/shard_map/ppermute | solution.py:229
  97.9 2.8 %collective-permute-start.39 = (bf16[256,256]{1,0:T(8,128)(2,1)S(1)}, bf16[256,256]{1,0:T(8,128)(2,1)S(1)}, u32[]{:S(2)}, u32[]{:S(2)}) collective-permute-start(bf16[256,256]{1,0:T(8,128)(2,1)S(1)} %get-tuple-element.78), channel_id=1, source_target_pairs={{0,6},{1,7},{2,0},{3,1},{4,2},{5,3},{6,4},{7,5},{8,14},{9,15},{10,... | collective-permute-start | bytes 393224 | tf_op jit(solution)/shard_map/ppermute | solution.py:232
  102.6 2.8 %collective-permute-start.37 = (bf16[256,256]{1,0:T(8,128)(2,1)S(1)}, bf16[256,256]{1,0:T(8,128)(2,1)S(1)}, u32[]{:S(2)}, u32[]{:S(2)}) collective-permute-start(bf16[256,256]{1,0:T(8,128)(2,1)S(1)} %add_convert_fusion.1), channel_id=1, source_target_pairs={{0,2},{1,3},{2,4},{3,5},{4,6},{5,7},{6,0},{7,1},{8,10},{9,11},{10,... | collective-permute-start | bytes 393224 | tf_op jit(solution)/shard_map/ppermute | solution.py:229
  105.4 4.7 %collective-permute-start.38 = (bf16[256,256]{1,0:T(8,128)(2,1)S(1)}, bf16[256,256]{1,0:T(8,128)(2,1)S(1)}, u32[]{:S(2)}, u32[]{:S(2)}) collective-permute-start(bf16[256,256]{1,0:T(8,128)(2,1)S(1)} %get-tuple-element.77), channel_id=1, source_target_pairs={{0,2},{1,3},{2,4},{3,5},{4,6},{5,7},{6,0},{7,1},{8,10},{9,11},{10,... | collective-permute-start | bytes 393224 | tf_op jit(solution)/shard_map/ppermute | solution.py:229
  110.1 2.1 %collective-permute-done.39 = bf16[256,256]{1,0:T(8,128)(2,1)S(1)} collective-permute-done((bf16[256,256]{1,0:T(8,128)(2,1)S(1)}, bf16[256,256]{1,0:T(8,128)(2,1)S(1)}, u32[]{:S(2)}, u32[]{:S(2)}) %collective-permute-start.39) | collective-permute-done | bytes 131104 | tf_op jit(solution)/shard_map/ppermute | solution.py:232
  112.4 2.4 %collective-permute-start.40 = (bf16[256,256]{1,0:T(8,128)(2,1)S(1)}, bf16[256,256]{1,0:T(8,128)(2,1)S(1)}, u32[]{:S(2)}, u32[]{:S(2)}) collective-permute-start(bf16[256,256]{1,0:T(8,128)(2,1)S(1)} %get-tuple-element.80), channel_id=1, source_target_pairs={{0,6},{1,7},{2,0},{3,1},{4,2},{5,3},{6,4},{7,5},{8,14},{9,15},{10,... | collective-permute-start | bytes 393224 | tf_op jit(solution)/shard_map/ppermute | solution.py:232
  114.8 3.4 %collective-permute-done.38 = bf16[256,256]{1,0:T(8,128)(2,1)S(1)} collective-permute-done((bf16[256,256]{1,0:T(8,128)(2,1)S(1)}, bf16[256,256]{1,0:T(8,128)(2,1)S(1)}, u32[]{:S(2)}, u32[]{:S(2)}) %collective-permute-start.38) | collective-permute-done | bytes 131104 | tf_op jit(solution)/shard_map/ppermute | solution.py:229
  118.1 6.6 %collective-permute-done.40 = bf16[256,256]{1,0:T(8,128)(2,1)S(1)} collective-permute-done((bf16[256,256]{1,0:T(8,128)(2,1)S(1)}, bf16[256,256]{1,0:T(8,128)(2,1)S(1)}, u32[]{:S(2)}, u32[]{:S(2)}) %collective-permute-start.40) | collective-permute-done | bytes 131104 | tf_op jit(solution)/shard_map/ppermute | solution.py:232
  (101 shorter events, 43.1 us)
Async XLA Ops:
  1.8 9.5 %collective-permute-start.4 = (bf16[512,256]{1,0:T(8,128)(2,1)S(1)}, bf16[512,256]{1,0:T(8,128)(2,1)S(1)}, u32[]{:S(2)}, u32[]{:S(2)}) collective-permute-start(bf16[512,256]{1,0:T(8,128)(2,1)S(1)} %multiply_convert_fusion.refs_0_), channel_id=1, source_target_pairs={{0,64},{8,72},{16,80},{24,88},{32,96},{40,104},{48,112},{56,120},{... | collective-permute-start | bytes 786440 | tf_op jit(solution)/shard_map/ppermute | solution.py:103
  8.1 18.3 %collective-permute-start.6 = (bf16[512,256]{1,0:T(8,128)(2,1)S(1)}, bf16[512,256]{1,0:T(8,128)(2,1)S(1)}, u32[]{:S(2)}, u32[]{:S(2)}) collective-permute-start(bf16[512,256]{1,0:T(8,128)(2,1)S(1)} %multiply_convert_fusion.refs_0_), channel_id=1, source_target_pairs={{0,16},{8,24},{16,32},{24,40},{32,48},{40,56},{48,0},{56,8},{64,80... | collective-permute-start | bytes 786440 | tf_op jit(solution)/shard_map/ppermute | solution.py:103
  9.6 14.2 %collective-permute-start.5 = (bf16[512,256]{1,0:T(8,128)(2,1)S(1)}, bf16[512,256]{1,0:T(8,128)(2,1)S(1)}, u32[]{:S(2)}, u32[]{:S(2)}) collective-permute-start(bf16[512,256]{1,0:T(8,128)(2,1)S(1)} %multiply_convert_fusion.refs_0_), channel_id=1, source_target_pairs={{0,192},{8,200},{16,208},{24,216},{32,224},{40,232},{48,240},{56,2... | collective-permute-start | bytes 786440 | tf_op jit(solution)/shard_map/ppermute | solution.py:103
  11.4 17.0 %collective-permute-start.7 = (bf16[512,256]{1,0:T(8,128)(2,1)S(1)}, bf16[512,256]{1,0:T(8,128)(2,1)S(1)}, u32[]{:S(2)}, u32[]{:S(2)}) collective-permute-start(bf16[512,256]{1,0:T(8,128)(2,1)S(1)} %collective-permute-done.3.refs_1_), channel_id=1, source_target_pairs={{0,48},{8,56},{16,0},{24,8},{32,16},{40,24},{48,32},{56,40},{64,11... | collective-permute-start | bytes 786440 | tf_op jit(solution)/shard_map/ppermute | solution.py:103
  12.6 17.0 %collective-permute-start.8 = (bf16[512,256]{1,0:T(8,128)(2,1)S(1)}, bf16[512,256]{1,0:T(8,128)(2,1)S(1)}, u32[]{:S(2)}, u32[]{:S(2)}) collective-permute-start(bf16[512,256]{1,0:T(8,128)(2,1)S(1)} %collective-permute-done.3.refs_1_), channel_id=1, source_target_pairs={{0,64},{8,72},{16,80},{24,88},{32,96},{40,104},{48,112},{56,120},{... | collective-permute-start | bytes 786440 | tf_op jit(solution)/shard_map/ppermute | solution.py:103
  36.2 9.6 %collective-permute-start.17 = (bf16[512,256]{1,0:T(8,128)(2,1)S(1)}, bf16[512,256]{1,0:T(8,128)(2,1)S(1)}, u32[]{:S(2)}, u32[]{:S(2)}) collective-permute-start(bf16[512,256]{1,0:T(8,128)(2,1)S(1)} %collective-permute-done.9.refs_7_), channel_id=1, source_target_pairs={{0,48},{8,56},{16,0},{24,8},{32,16},{40,24},{48,32},{56,40},{64,11... | collective-permute-start | bytes 786440 | tf_op jit(solution)/shard_map/ppermute | solution.py:103
  40.6 9.7 %collective-permute-start.19 = (bf16[512,256]{1,0:T(8,128)(2,1)S(1)}, bf16[512,256]{1,0:T(8,128)(2,1)S(1)}, u32[]{:S(2)}, u32[]{:S(2)}) collective-permute-start(bf16[512,256]{1,0:T(8,128)(2,1)S(1)} %collective-permute-done.14.refs_12_), channel_id=1, source_target_pairs={{0,192},{8,200},{16,208},{24,216},{32,224},{40,232},{48,240},{56,2... | collective-permute-start | bytes 786440 | tf_op jit(solution)/shard_map/ppermute | solution.py:103
  40.6 10.4 %collective-permute-start.21 = (bf16[512,256]{1,0:T(8,128)(2,1)S(1)}, bf16[512,256]{1,0:T(8,128)(2,1)}, u32[]{:S(2)}, u32[]{:S(2)}) collective-permute-start(bf16[512,256]{1,0:T(8,128)(2,1)S(1)} %collective-permute-done.14.refs_12_), channel_id=1, source_target_pairs={{0,8},{8,0},{16,24},{24,16},{32,40},{40,32},{48,56},{56,48},{64,72... | collective-permute-start | bytes 786440 | tf_op jit(solution)/shard_map/ppermute | solution.py:103
  42.5 9.7 %collective-permute-start.20 = (bf16[512,256]{1,0:T(8,128)(2,1)S(1)}, bf16[512,256]{1,0:T(8,128)(2,1)S(1)}, u32[]{:S(2)}, u32[]{:S(2)}) collective-permute-start(bf16[512,256]{1,0:T(8,128)(2,1)S(1)} %collective-permute-done.11.refs_9_), channel_id=1, source_target_pairs={{0,16},{8,24},{16,32},{24,40},{32,48},{40,56},{48,0},{56,8},{64,80... | collective-permute-start | bytes 786440 | tf_op jit(solution)/shard_map/ppermute | solution.py:103
  51.0 11.2 %collective-permute-start.24 = (bf16[512,256]{1,0:T(8,128)(2,1)S(1)}, bf16[512,256]{1,0:T(8,128)(2,1)}, u32[]{:S(2)}, u32[]{:S(2)}) collective-permute-start(bf16[512,256]{1,0:T(8,128)(2,1)S(1)} %collective-permute-done.11.refs_9_), channel_id=1, source_target_pairs={{0,192},{8,200},{16,208},{24,216},{32,224},{40,232},{48,240},{56,2... | collective-permute-start | bytes 786440 | tf_op jit(solution)/shard_map/ppermute | solution.py:103
  51.0 11.2 %collective-permute-start.26 = (bf16[512,256]{1,0:T(8,128)(2,1)S(1)}, bf16[512,256]{1,0:T(8,128)(2,1)}, u32[]{:S(2)}, u32[]{:S(2)}) collective-permute-start(bf16[512,256]{1,0:T(8,128)(2,1)S(1)} %collective-permute-done.6.refs_4_), channel_id=1, source_target_pairs={{0,8},{8,0},{16,24},{24,16},{32,40},{40,32},{48,56},{56,48},{64,72... | collective-permute-start | bytes 786440 | tf_op jit(solution)/shard_map/ppermute | solution.py:103
  52.8 10.2 %collective-permute-start.25 = (bf16[512,256]{1,0:T(8,128)(2,1)}, bf16[512,256]{1,0:T(8,128)(2,1)}, u32[]{:S(2)}, u32[]{:S(2)}) collective-permute-start(bf16[512,256]{1,0:T(8,128)(2,1)} %collective-permute-done.16.refs_14_), channel_id=1, source_target_pairs={{0,16},{8,24},{16,32},{24,40},{32,48},{40,56},{48,0},{56,8},{64,80... | collective-permute-start | bytes 786440 | tf_op jit(solution)/shard_map/ppermute | solution.py:103
  56.5 10.1 %collective-permute-start.28 = (bf16[512,256]{1,0:T(8,128)(2,1)}, bf16[512,256]{1,0:T(8,128)(2,1)}, u32[]{:S(2)}, u32[]{:S(2)}) collective-permute-start(bf16[512,256]{1,0:T(8,128)(2,1)} %collective-permute-done.21.refs_19_), channel_id=1, source_target_pairs={{0,64},{8,72},{16,80},{24,88},{32,96},{40,104},{48,112},{56,120},{... | collective-permute-start | bytes 786440 | tf_op jit(solution)/shard_map/ppermute | solution.py:103
  62.1 23.1 %collective-permute-start.31 = (bf16[512,256]{1,0:T(8,128)(2,1)}, bf16[512,256]{1,0:T(8,128)(2,1)S(1)}, u32[]{:S(2)}, u32[]{:S(2)}) collective-permute-start(bf16[512,256]{1,0:T(8,128)(2,1)} %collective-permute-done.22.refs_20_), channel_id=1, source_target_pairs={{0,192},{8,200},{16,208},{24,216},{32,224},{40,232},{48,240},{56,2... | collective-permute-start | bytes 786440 | tf_op jit(solution)/shard_map/ppermute | solution.py:103
  62.1 23.1 %collective-permute-start.30 = (bf16[512,256]{1,0:T(8,128)(2,1)S(1)}, bf16[512,256]{1,0:T(8,128)(2,1)S(1)}, u32[]{:S(2)}, u32[]{:S(2)}) collective-permute-start(bf16[512,256]{1,0:T(8,128)(2,1)S(1)} %collective-permute-done.12.refs_10_), channel_id=1, source_target_pairs={{0,8},{8,0},{16,24},{24,16},{32,40},{40,32},{48,56},{56,48},{64,72... | collective-permute-start | bytes 786440 | tf_op jit(solution)/shard_map/ppermute | solution.py:103
  63.1 22.2 %collective-permute-start.29 = (bf16[512,256]{1,0:T(8,128)(2,1)}, bf16[512,256]{1,0:T(8,128)(2,1)S(1)}, u32[]{:S(2)}, u32[]{:S(2)}) collective-permute-start(bf16[512,256]{1,0:T(8,128)(2,1)} %copy-done.8), channel_id=1, source_target_pairs={{0,16},{8,24},{16,32},{24,40},{32,48},{40,56},{48,0},{56,8},{64,80... | collective-permute-start | bytes 786440 | tf_op jit(solution)/shard_map/ppermute | solution.py:103
  66.6 18.7 %collective-permute-start.33 = (bf16[512,256]{1,0:T(8,128)(2,1)}, bf16[512,256]{1,0:T(8,128)(2,1)S(1)}, u32[]{:S(2)}, u32[]{:S(2)}) collective-permute-start(bf16[512,256]{1,0:T(8,128)(2,1)} %collective-permute-done.27.refs_25_), channel_id=1, source_target_pairs={{0,64},{8,72},{16,80},{24,88},{32,96},{40,104},{48,112},{56,120},{... | collective-permute-start | bytes 786440 | tf_op jit(solution)/shard_map/ppermute | solution.py:103
  70.3 15.0 %collective-permute-start.32 = (bf16[512,256]{1,0:T(8,128)(2,1)}, bf16[512,256]{1,0:T(8,128)(2,1)S(1)}, u32[]{:S(2)}, u32[]{:S(2)}) collective-permute-start(bf16[512,256]{1,0:T(8,128)(2,1)} %copy-done.8), channel_id=1, source_target_pairs={{0,48},{8,56},{16,0},{24,8},{32,16},{40,24},{48,32},{56,40},{64,11... | collective-permute-start | bytes 786440 | tf_op jit(solution)/shard_map/ppermute | solution.py:103
  93.1 9.5 %collective-permute-start.36 = (bf16[256,256]{1,0:T(8,128)(2,1)S(1)}, bf16[256,256]{1,0:T(8,128)(2,1)S(1)}, u32[]{:S(2)}, u32[]{:S(2)}) collective-permute-start(bf16[256,256]{1,0:T(8,128)(2,1)S(1)} %get-tuple-element.76), channel_id=1, source_target_pairs={{0,2},{1,3},{2,4},{3,5},{4,6},{5,7},{6,0},{7,1},{8,10},{9,11},{10,... | collective-permute-start | bytes 393224 | tf_op jit(solution)/shard_map/ppermute | solution.py:229
  96.2 13.9 %collective-permute-start.35 = (bf16[256,256]{1,0:T(8,128)(2,1)S(1)}, bf16[256,256]{1,0:T(8,128)(2,1)S(1)}, u32[]{:S(2)}, u32[]{:S(2)}) collective-permute-start(bf16[256,256]{1,0:T(8,128)(2,1)S(1)} %get-tuple-element.75), channel_id=1, source_target_pairs={{0,6},{1,7},{2,0},{3,1},{4,2},{5,3},{6,4},{7,5},{8,14},{9,15},{10,... | collective-permute-start | bytes 393224 | tf_op jit(solution)/shard_map/ppermute | solution.py:232
  97.9 14.3 %collective-permute-start.39 = (bf16[256,256]{1,0:T(8,128)(2,1)S(1)}, bf16[256,256]{1,0:T(8,128)(2,1)S(1)}, u32[]{:S(2)}, u32[]{:S(2)}) collective-permute-start(bf16[256,256]{1,0:T(8,128)(2,1)S(1)} %get-tuple-element.78), channel_id=1, source_target_pairs={{0,6},{1,7},{2,0},{3,1},{4,2},{5,3},{6,4},{7,5},{8,14},{9,15},{10,... | collective-permute-start | bytes 393224 | tf_op jit(solution)/shard_map/ppermute | solution.py:232
  102.6 9.6 %collective-permute-start.37 = (bf16[256,256]{1,0:T(8,128)(2,1)S(1)}, bf16[256,256]{1,0:T(8,128)(2,1)S(1)}, u32[]{:S(2)}, u32[]{:S(2)}) collective-permute-start(bf16[256,256]{1,0:T(8,128)(2,1)S(1)} %add_convert_fusion.1), channel_id=1, source_target_pairs={{0,2},{1,3},{2,4},{3,5},{4,6},{5,7},{6,0},{7,1},{8,10},{9,11},{10,... | collective-permute-start | bytes 393224 | tf_op jit(solution)/shard_map/ppermute | solution.py:229
  105.4 12.7 %collective-permute-start.38 = (bf16[256,256]{1,0:T(8,128)(2,1)S(1)}, bf16[256,256]{1,0:T(8,128)(2,1)S(1)}, u32[]{:S(2)}, u32[]{:S(2)}) collective-permute-start(bf16[256,256]{1,0:T(8,128)(2,1)S(1)} %get-tuple-element.77), channel_id=1, source_target_pairs={{0,2},{1,3},{2,4},{3,5},{4,6},{5,7},{6,0},{7,1},{8,10},{9,11},{10,... | collective-permute-start | bytes 393224 | tf_op jit(solution)/shard_map/ppermute | solution.py:229
  112.4 12.3 %collective-permute-start.40 = (bf16[256,256]{1,0:T(8,128)(2,1)S(1)}, bf16[256,256]{1,0:T(8,128)(2,1)S(1)}, u32[]{:S(2)}, u32[]{:S(2)}) collective-permute-start(bf16[256,256]{1,0:T(8,128)(2,1)S(1)} %get-tuple-element.80), channel_id=1, source_target_pairs={{0,6},{1,7},{2,0},{3,1},{4,2},{5,3},{6,4},{7,5},{8,14},{9,15},{10,... | collective-permute-start | bytes 393224 | tf_op jit(solution)/shard_map/ppermute | solution.py:232
  (31 other events, 180.6 us)

commit v3 on v2

v3 whole, which is shorter than its diff:
```python
import functools

import jax
import jax.numpy as jnp
from jax import lax
from jax.experimental import pallas as pl
from jax.experimental.pallas import tpu as pltpu
from jax.sharding import PartitionSpec as P

NX, NY, NZ = 4, 4, 2
NH = 4
PANEL = 512
BLOCK = 128
F = 256
RB = 32
MAXB = 11
KPER = PANEL // BLOCK
SHARDS = NX * NY * NZ
STOPS = (9, 18, 27)
KERNEL_VMEM = 16 << 20
EARLY_VMEM = 36 << 20
HIDDEN = pltpu.VMEM((SHARDS * PANEL + BLOCK, F), jnp.bfloat16)
ADJ = pltpu.VMEM((RB // 2, MAXB, BLOCK, BLOCK), jnp.bfloat16)

PLAN = (
    (0, -1, ((0, 0, 0),)),
    (0, 1, ((0, 0, 0),)),
    (1, -1, ((0, 0, 0),)),
    (1, 1, ((0, 0, 0),)),
    (2, 1, ((0, 0, 0),)),
    (0, -1, ((0, 1, 0),)),
    (0, 1, ((0, 3, 0),)),
    (1, -1, ((3, 0, 0),)),
    (1, 1, ((0, 0, 1),)),
    (2, 1, ((1, 0, 0),)),
    (0, 1, ((1, 0, 0),)),
    (1, -1, ((0, 0, 1),)),
    (1, 1, ((0, 1, 0),)),
    (2, 1, ((3, 0, 0),)),
    (0, -1, ((0, 1, 1),)),
    (0, 1, ((0, 1, 0),)),
    (1, -1, ((3, 3, 0),)),
    (1, 1, ((0, 1, 1),)),
    (2, 1, ((1, 3, 0),)),
    (0, -1, ((3, 1, 0),)),
    (0, 1, ((0, 2, 0),)),
    (1, -1, ((2, 0, 0),)),
    (1, 1, ((1, 0, 1),)),
    (2, 1, ((2, 0, 0),)),
    (0, -1, ((3, 1, 1),)),
    (0, 1, ((1, 3, 1),)),
    (1, -1, ((1, 3, 1),)),
    (1, 1, ((2, 1, 0),)),
    (2, 1, ((3, 3, 0),)),
    (0, -1, ((0, 2, 1),)),
    (1, 1, ((2, 1, 1),)),
)
LATE = (25, 26, 28, 29, 30)


def row_perm(axis, step):
    pairs = []
    for y in range(NY):
        for x in range(NX):
            for z in range(NZ):
                c = [x, y, z]
                c[axis] = (c[axis] + step) % (NX, NY, NZ)[axis]
                pairs.append(((y * NX + x) * NZ + z, (c[1] * NX + c[0]) * NZ + c[2]))
    return pairs


def col_perm(dz, core):
    return [(h * 2 + c, ((h + dz) % NH) * 2 + (c ^ core)) for h in range(NH) for c in range(2)]


def after(value, *others):
    return lax.optimization_barrier((value, *others))[0]


def moved(place, axis, step):
    place = list(place)
    place[axis] = (place[axis] + step) % (NX, NY, NZ)[axis]
    return tuple(place)


def gather_rows(mine):
    arrays, at, last = [(mine, ((0, 0, 0),))], {(0, 0, 0): (0, 0)}, {}
    for axis, step, sources in PLAN:
        index = at[sources[0]][0]
        if arrays[index][1] == sources:
            value = arrays[index][0]
        else:
            rows = []
            for source in sources:
                index, n = at[source]
                array = arrays[index][0]
                rows.append(array if len(arrays[index][1]) == 1 else array[n * PANEL : (n + 1) * PANEL])
            value = rows[0] if len(rows) == 1 else jnp.concatenate(rows)
        link = (axis, step)
        if link in last:
            value = after(value, last[link])
        last[link] = got = lax.ppermute(value, "row", row_perm(axis, step))
        places = tuple(moved(source, axis, step) for source in sources)
        for n, place in enumerate(places):
            at[place] = (len(arrays), n)
        arrays.append((got, places))
    return arrays


def gather_weight(weight):
    pair = jnp.concatenate([weight, lax.ppermute(weight, "col", col_perm(0, 1))])
    return [pair] + [lax.ppermute(pair, "col", col_perm(d, 0)) for d in range(1, NH)]


def hidden_rows(pieces, weight, hidden, at):
    for piece in pieces:
        rows = pl.ds(at, piece.shape[0])
        hidden[rows, :] = jnp.dot(piece[...], weight[...], preferred_element_type=jnp.float32).astype(jnp.bfloat16)
        at += piece.shape[0]


def adjacency_copies(col, side, adj_hbm, adj, sems):
    chip, core = lax.shift_right_logical(col, 1), (col & 1) ^ side
    copies = []
    for d in range(NH):
        panel = ((chip + d) & (NH - 1)) * 2 + core
        source = adj_hbm.at[pl.ds(panel * KPER, KPER), 0]
        copies.append(pltpu.make_async_copy(source, adj.at[pl.ds(d * KPER, KPER)], sems.at[d]))
    return copies


def early_kernel(here_ref, adj_hbm, *refs):
    pairs, (*pieces, hidden, adj, weight, sems, weight_sems, piece_sems) = refs[:NH], refs[NH:]
    piece_copies = [
        pltpu.make_async_copy(piece, hidden.at[pl.ds(n * PANEL, PANEL)], piece_sems.at[n])
        for n, piece in enumerate(pieces)
    ]
    rows = F // (NH * 2)
    col = here_ref[1]
    weight_copies = []
    for n in range(NH * 2):
        place = ((lax.shift_right_logical(col, 1) - n // 2) & (NH - 1)) * 2 + ((col & 1) ^ (n % 2))
        source = pairs[n // 2].at[pl.ds(n % 2 * rows, rows)]
        target = weight.at[pl.ds(pl.multiple_of(place * rows, rows), rows)]
        weight_copies.append(pltpu.make_async_copy(source, target, weight_sems.at[n]))
    copies = adjacency_copies(here_ref[1], 1, adj_hbm, adj, sems)
    for copy in weight_copies + piece_copies + copies:
        copy.start()
    hidden[pl.ds(SHARDS * PANEL, BLOCK), :] = jnp.zeros((BLOCK, F), jnp.bfloat16)
    for copy in weight_copies:
        copy.wait()
    for n, copy in enumerate(piece_copies):
        copy.wait()
        if n + 1 in STOPS:
            first = max([0] + [stop for stop in STOPS if stop <= n])
            rows = pl.ds(first * PANEL, (n + 1 - first) * PANEL)
            hidden[rows, :] = jnp.dot(hidden[rows, :], weight[...], preferred_element_type=jnp.float32).astype(
                jnp.bfloat16
            )
    for copy in copies:
        copy.wait()


def early(here, pairs, adjacency, pieces):
    smem, vmem, anywhere = (pl.BlockSpec(memory_space=m) for m in (pltpu.SMEM, pltpu.VMEM, pl.ANY))
    return pl.pallas_call(
        early_kernel,
        in_specs=[smem, anywhere] + [anywhere] * (len(pairs) + len(pieces)),
        out_specs=[vmem, vmem, vmem],
        scratch_shapes=[pltpu.SemaphoreType.DMA((n,)) for n in (NH, NH * 2, len(pieces))],
        out_shape=[HIDDEN, ADJ, pltpu.VMEM((F, F), jnp.bfloat16)],
        compiler_params=pltpu.CompilerParams(vmem_limit_bytes=EARLY_VMEM),
        cost_estimate=pl.CostEstimate(flops=2 * 13000 * F * F, bytes_accessed=20 << 20, transcendentals=0),
    )(here, adjacency, *pairs, *pieces)


def products(here_ref, index_ref, count_ref, hidden, adj, table, order, side, out_ref):
    row, col = here_ref[0], here_ref[1]
    y, x, z = lax.shift_right_logical(row, 3), lax.shift_right_logical(row, 1) & (NX - 1), row & (NZ - 1)
    chip, core = lax.shift_right_logical(col, 1), (col & 1) ^ side
    for n, (dx, dy, dz) in enumerate(order):
        shard = (((y - dy) & (NY - 1)) * NX + ((x - dx) & (NX - 1))) * NZ + (z ^ dz)
        table[shard] = n * PANEL

    def rows_at(block, m):
        column = index_ref[block, 0, m]
        start = table[lax.shift_right_logical(column, 2)] + (column & (KPER - 1)) * BLOCK
        start = jnp.where(m < count_ref[block, 0], start, SHARDS * PANEL)
        return hidden[pl.ds(pl.multiple_of(start, BLOCK), BLOCK), :]

    def total_of(block, at):
        right = [rows_at(block, m) for m in range(MAXB)]
        left = [adj[at, m] for m in range(MAXB)]
        return jnp.dot(
            jnp.concatenate(left, axis=1), jnp.concatenate(right, axis=0), preferred_element_type=jnp.float32
        )

    def body(d, _):
        panel = ((chip + d) & (NH - 1)) * 2 + core
        for j in range(KPER):
            at = pl.ds(pl.multiple_of(d * PANEL + j * BLOCK, BLOCK), BLOCK)
            out_ref[at, :] = total_of(panel * KPER + j, d * KPER + j).astype(out_ref.dtype)
        return 0

    lax.fori_loop(0, NH, body, 0)


def send_kernel(order, here_ref, index_ref, count_ref, hidden_in, adj, adj_hbm, weight, *refs):
    *pieces, send_ref, hidden, next_adj, table, sems = refs
    del hidden_in
    copies = adjacency_copies(here_ref[1], 0, adj_hbm, next_adj, sems)
    for copy in copies:
        copy.start()
    hidden_rows(pieces, weight, hidden, SHARDS * PANEL - sum(piece.shape[0] for piece in pieces))
    products(here_ref, index_ref, count_ref, hidden, adj, table, order, 1, send_ref)
    for copy in copies:
        copy.wait()


def keep_kernel(order, here_ref, index_ref, count_ref, hidden, adj, keep_ref, table):
    products(here_ref, index_ref, count_ref, hidden, adj, table, order, 0, keep_ref)


def send_products(order, here, index, counts, hidden, adj, adjacency, weight, pieces):
    smem, vmem, anywhere = (pl.BlockSpec(memory_space=m) for m in (pltpu.SMEM, pltpu.VMEM, pl.ANY))
    return pl.pallas_call(
        functools.partial(send_kernel, order),
        in_specs=[smem, smem, smem, vmem, vmem, anywhere, vmem] + [vmem] * len(pieces),
        out_specs=[vmem, vmem, vmem],
        scratch_shapes=[pltpu.SMEM((SHARDS,), jnp.int32), pltpu.SemaphoreType.DMA((NH,))],
        out_shape=[pltpu.VMEM((NH * PANEL, F), jnp.bfloat16), HIDDEN, ADJ],
        input_output_aliases={3: 1},
        compiler_params=pltpu.CompilerParams(vmem_limit_bytes=KERNEL_VMEM),
        cost_estimate=pl.CostEstimate(flops=1500000000, bytes_accessed=8 << 20, transcendentals=0),
    )(here, index, counts, hidden, adj, adjacency, weight, *pieces)


def keep_products(order, here, index, counts, hidden, adj):
    smem, vmem = (pl.BlockSpec(memory_space=m) for m in (pltpu.SMEM, pltpu.VMEM))
    return pl.pallas_call(
        functools.partial(keep_kernel, order),
        in_specs=[smem, smem, smem, vmem, vmem],
        out_specs=vmem,
        scratch_shapes=[pltpu.SMEM((SHARDS,), jnp.int32)],
        out_shape=pltpu.VMEM((NH * PANEL, F), jnp.float32),
        compiler_params=pltpu.CompilerParams(vmem_limit_bytes=KERNEL_VMEM),
        cost_estimate=pl.CostEstimate(flops=1500000000, bytes_accessed=8 << 20, transcendentals=0),
    )(here, index, counts, hidden, adj)


def reduce_chips(got, keep):
    h = PANEL // 2

    def part(d, side):
        at = d * PANEL + side * h
        return keep[at : at + h] + got[at : at + h].astype(jnp.float32)

    def plus(value):
        return lax.ppermute(value.astype(jnp.bfloat16), "col", col_perm(1, 0)).astype(jnp.float32)

    def minus(value):
        return lax.ppermute(value.astype(jnp.bfloat16), "col", col_perm(-1, 0)).astype(jnp.float32)

    first = [part(2, 0), part(2, 1), part(1, 1), part(3, 0)]
    first = lax.optimization_barrier([value.astype(jnp.bfloat16) for value in first])
    far_top, far_bottom = plus(first[0]), minus(first[1])
    near_bottom, near_top = plus(first[2]), minus(first[3])
    chain_top = plus(part(1, 0) + far_top)
    chain_bottom = minus(part(3, 1) + far_bottom)
    top = part(0, 0) + near_top + chain_top
    bottom = part(0, 1) + near_bottom + chain_bottom
    return jnp.concatenate([top, bottom])


def on_device(
    feature_codes,
    bit_widths,
    row_scales,
    weight,
    layer_bias,
    adjacency_blocks,
    block_index,
    block_counts,
):
    here = jnp.stack([lax.axis_index("row"), lax.axis_index("col")]).astype(jnp.int32)
    shift = 8 - bit_widths[0]
    level = jnp.left_shift(jnp.right_shift(feature_codes, shift), shift)
    features = (level.astype(jnp.float32) * row_scales[:, None]).astype(jnp.bfloat16)
    pairs = gather_weight(weight)
    arrays = gather_rows(features)

    soon = [a for n, a in enumerate(arrays) if n - 1 not in LATE]
    last = [arrays[n + 1] for n in LATE]
    order = [place for _, places in soon + last for place in places]
    blocks = pltpu.with_memory_space_constraint(adjacency_blocks, pltpu.HBM)
    pieces = [pltpu.with_memory_space_constraint(a, pltpu.HBM) for a, _ in soon]
    hidden, adj, full_weight = early(here, pairs, blocks, pieces)
    tables = (here, block_index, block_counts)
    send, hidden, adj = send_products(order, *tables, hidden, adj, blocks, full_weight, [a for a, _ in last])
    got = lax.ppermute(send, "col", col_perm(0, 1))
    keep = keep_products(order, *tables, hidden, adj)
    summed = reduce_chips(got, keep)
    return jnp.maximum(summed + layer_bias[None, :], 0.0).astype(jnp.bfloat16)


def solution(mesh):
    in_specs = (
        P(("row", "col"), None),
        P(("row", "col")),
        P(("row", "col")),
        P("col", None),
        P(),
        P("row", "col", None, None, None),
        P("row", "col", None),
        P("row", "col"),
    )
    out_specs = P(("row", "col"), None)
    return jax.shard_map(
        on_device, mesh=mesh, in_specs=in_specs, out_specs=out_specs, check_vma=False
    )
```

time: 126 us -> 110 us (0.87)
  the two profiles are of different devices: /device:TPU:26 before, /device:TPU:38 now
where the time goes in v3:
time: 110 us; the launch traced here: 109 us
  starting transfers between devices  55.6 us (51%)
  waiting for transfers between devices  33.6 us (31%)
  Pallas kernels  14.1 us (13%)
  local copies, waits for them, and re-layouts  2.32 us (2%)
  other arithmetic  2.31 us (2%)
    ppermute x31, starting transfers between devices, gather_rows(): last[link] = got = lax.ppermute(value, 'row', row_perm(axis, step))  37.9 us
    ppermute x3, waiting for transfers between devices, plus(): lax.ppermute(value.astype(jnp.bfloat16), 'col', col_perm(1, 0))  15.7 us
    ppermute x31, waiting for transfers between devices, gather_rows(): last[link] = got = lax.ppermute(value, 'row', row_perm(axis, step))  14.1 us
    ppermute x3, starting transfers between devices, gather_weight(): lax.ppermute(pair, 'col', col_perm(d, 0))  8.67 us
    pallas_call x1, Pallas kernels, early(): pl.pallas_call(early_kernel, in_specs=[smem, anywhere] + [anywhere] * (le...  6.33 us
    ppermute x3, starting transfers between devices, plus(): lax.ppermute(value.astype(jnp.bfloat16), 'col', col_perm(1, 0))  6.12 us
    pallas_call x1, Pallas kernels, send_products(): pl.pallas_call(functools.partial(send_kernel, order), in_specs=[smem, sme...  4.17 us
    ppermute x3, waiting for transfers between devices, minus(): lax.ppermute(value.astype(jnp.bfloat16), 'col', col_perm(-1, 0))  3.77 us
  transfers between devices with their start and end apart: 42, of which 16 were waited for; matrix products, arithmetic and copies ran while one was open for 2% of the time, Pallas kernels for 9%

profile of v3, /device:TPU:38, one launch (start us, length us, event | category | flops | bytes accessed | tf_op | source)
XLA Modules:
  0.0 109.0 jit_solution(15635364934883431333)
XLA Ops:
  3.6 1.7 %collective-permute-start.6 = (bf16[512,256]{1,0:T(8,128)(2,1)S(1)}, bf16[512,256]{1,0:T(8,128)(2,1)S(1)}, u32[]{:S(2)}, u32[]{:S(2)}) collective-permute-start(bf16[512,256]{1,0:T(8,128)(2,1)S(1)} %multiply_convert_fusion.refs_4_), channel_id=1, source_target_pairs={{0,192},{8,200},{16,208},{24,216},{32,224},{40,232},{48,240},{56,2... | collective-permute-start | bytes 786440 | tf_op jit(solution)/shard_map/ppermute | solution.py:102
  5.3 2.2 %collective-permute-start.5 = (bf16[512,256]{1,0:T(8,128)(2,1)S(1)}, bf16[512,256]{1,0:T(8,128)(2,1)S(1)}, u32[]{:S(2)}, u32[]{:S(2)}) collective-permute-start(bf16[512,256]{1,0:T(8,128)(2,1)S(1)} %multiply_convert_fusion.refs_4_), channel_id=1, source_target_pairs={{0,16},{8,24},{16,32},{24,40},{32,48},{40,56},{48,0},{56,8},{64,80... | collective-permute-start | bytes 786440 | tf_op jit(solution)/shard_map/ppermute | solution.py:102
  7.5 2.5 %collective-permute-done.8.refs_9_ = bf16[512,256]{1,0:T(8,128)(2,1)S(1)} collective-permute-done((bf16[512,256]{1,0:T(8,128)(2,1)S(1)}, bf16[512,256]{1,0:T(8,128)(2,1)S(1)}, u32[]{:S(2)}, u32[]{:S(2)}) %collective-permute-start.8) | collective-permute-done | bytes 262176 | tf_op jit(solution)/shard_map/ppermute | solution.py:102
  12.9 2.2 %collective-permute-start.10 = (bf16[512,256]{1,0:T(8,128)(2,1)S(1)}, bf16[512,256]{1,0:T(8,128)(2,1)S(1)}, u32[]{:S(2)}, u32[]{:S(2)}) collective-permute-start(bf16[512,256]{1,0:T(8,128)(2,1)S(1)} %collective-permute-done.6.refs_7_), channel_id=1, source_target_pairs={{0,16},{8,24},{16,32},{24,40},{32,48},{40,56},{48,0},{56,8},{64,80... | collective-permute-start | bytes 786440 | tf_op jit(solution)/shard_map/ppermute | solution.py:102
  19.8 3.0 %collective-permute-start.14 = (bf16[512,256]{1,0:T(8,128)(2,1)S(1)}, bf16[512,256]{1,0:T(8,128)(2,1)}, u32[]{:S(2)}, u32[]{:S(2)}) collective-permute-start(bf16[512,256]{1,0:T(8,128)(2,1)S(1)} %collective-permute-done.5.refs_6_), channel_id=1, source_target_pairs={{0,16},{8,24},{16,32},{24,40},{32,48},{40,56},{48,0},{56,8},{64,80... | collective-permute-start | bytes 786440 | tf_op jit(solution)/shard_map/ppermute | solution.py:102
  23.1 1.9 %collective-permute-start.15 = (bf16[512,256]{1,0:T(8,128)(2,1)S(1)}, bf16[512,256]{1,0:T(8,128)(2,1)S(1)}, u32[]{:S(2)}, u32[]{:S(2)}) collective-permute-start(bf16[512,256]{1,0:T(8,128)(2,1)S(1)} %collective-permute-done.8.refs_9_), channel_id=1, source_target_pairs={{0,192},{8,200},{16,208},{24,216},{32,224},{40,232},{48,240},{56,2... | collective-permute-start | bytes 786440 | tf_op jit(solution)/shard_map/ppermute | solution.py:102
  27.9 3.8 %collective-permute-start.19 = (bf16[512,256]{1,0:T(8,128)(2,1)S(1)}, bf16[512,256]{1,0:T(8,128)(2,1)S(1)}, u32[]{:S(2)}, u32[]{:S(2)}) collective-permute-start(bf16[512,256]{1,0:T(8,128)(2,1)S(1)} %collective-permute-done.7.refs_8_), channel_id=1, source_target_pairs={{0,16},{8,24},{16,32},{24,40},{32,48},{40,56},{48,0},{56,8},{64,80... | collective-permute-start | bytes 786440 | tf_op jit(solution)/shard_map/ppermute | solution.py:102
  35.0 3.0 %collective-permute-done.19.refs_20_ = bf16[512,256]{1,0:T(8,128)(2,1)S(1)} collective-permute-done((bf16[512,256]{1,0:T(8,128)(2,1)S(1)}, bf16[512,256]{1,0:T(8,128)(2,1)S(1)}, u32[]{:S(2)}, u32[]{:S(2)}) %collective-permute-start.19) | collective-permute-done | bytes 262176 | tf_op jit(solution)/shard_map/ppermute | solution.py:102
  38.0 3.7 %collective-permute-start.24 = (bf16[512,256]{1,0:T(8,128)(2,1)S(1)}, bf16[512,256]{1,0:T(8,128)(2,1)S(1)}, u32[]{:S(2)}, u32[]{:S(2)}) collective-permute-start(bf16[512,256]{1,0:T(8,128)(2,1)S(1)} %collective-permute-done.16.refs_17_), channel_id=1, source_target_pairs={{0,16},{8,24},{16,32},{24,40},{32,48},{40,56},{48,0},{56,8},{64,80... | collective-permute-start | bytes 786440 | tf_op jit(solution)/shard_map/ppermute | solution.py:102
  42.6 1.9 %collective-permute-start.27 = (bf16[512,256]{1,0:T(8,128)(2,1)}, bf16[512,256]{1,0:T(8,128)(2,1)}, u32[]{:S(2)}, u32[]{:S(2)}) collective-permute-start(bf16[512,256]{1,0:T(8,128)(2,1)} %collective-permute-done.14.refs_15_), channel_id=1, source_target_pairs={{0,8},{8,0},{16,24},{24,16},{32,40},{40,32},{48,56},{56,48},{64,72... | collective-permute-start | bytes 786440 | tf_op jit(solution)/shard_map/ppermute | solution.py:102
  46.1 4.8 %collective-permute-start.3 = (bf16[64,256]{1,0:T(8,128)(2,1)S(1)}, bf16[64,256]{1,0:T(8,128)(2,1)S(1)}, u32[]{:S(2)}, u32[]{:S(2)}) collective-permute-start(bf16[64,256]{1,0:T(8,128)(2,1)S(1)} %constant_dynamic-update-slice_fusion.refs_0_), channel_id=1, source_target_pairs={{0,6},{1,7},{2,0},{3,1},{4,2},{5,3},{6,4},{7,5},{8,14},{9,15},{10,... | collective-permute-start | bytes 98312 | tf_op jit(solution)/shard_map/ppermute | solution.py:112
  50.9 2.0 %collective-permute-start.2 = (bf16[64,256]{1,0:T(8,128)(2,1)S(1)}, bf16[64,256]{1,0:T(8,128)(2,1)S(1)}, u32[]{:S(2)}, u32[]{:S(2)}) collective-permute-start(bf16[64,256]{1,0:T(8,128)(2,1)S(1)} %constant_dynamic-update-slice_fusion.refs_0_), channel_id=1, source_target_pairs={{0,4},{1,5},{2,6},{3,7},{4,0},{5,1},{6,2},{7,3},{8,12},{9,13},{10,... | collective-permute-start | bytes 98312 | tf_op jit(solution)/shard_map/ppermute | solution.py:112
  52.9 1.9 %collective-permute-start.1 = (bf16[64,256]{1,0:T(8,128)(2,1)S(1)}, bf16[64,256]{1,0:T(8,128)(2,1)S(1)}, u32[]{:S(2)}, u32[]{:S(2)}) collective-permute-start(bf16[64,256]{1,0:T(8,128)(2,1)S(1)} %constant_dynamic-update-slice_fusion.refs_0_), channel_id=1, source_target_pairs={{0,2},{1,3},{2,4},{3,5},{4,6},{5,7},{6,0},{7,1},{8,10},{9,11},{10,... | collective-permute-start | bytes 98312 | tf_op jit(solution)/shard_map/ppermute | solution.py:112
  58.2 2.4 %collective-permute-start.30 = (bf16[512,256]{1,0:T(8,128)(2,1)}, bf16[512,256]{1,0:T(8,128)(2,1)S(1)}, u32[]{:S(2)}, u32[]{:S(2)}) collective-permute-start(bf16[512,256]{1,0:T(8,128)(2,1)} %copy-done.16), channel_id=1, source_target_pairs={{0,16},{8,24},{16,32},{24,40},{32,48},{40,56},{48,0},{56,8},{64,80... | collective-permute-start | bytes 786440 | tf_op jit(solution)/shard_map/ppermute | solution.py:102
  60.6 3.2 %collective-permute-start.31 = (bf16[512,256]{1,0:T(8,128)(2,1)}, bf16[512,256]{1,0:T(8,128)(2,1)S(1)}, u32[]{:S(2)}, u32[]{:S(2)}) collective-permute-start(bf16[512,256]{1,0:T(8,128)(2,1)} %copy-done.16), channel_id=1, source_target_pairs={{0,192},{8,200},{16,208},{24,216},{32,224},{40,232},{48,240},{56,2... | collective-permute-start | bytes 786440 | tf_op jit(solution)/shard_map/ppermute | solution.py:102
  64.0 6.3 %shard_map.82 = (bf16[16512,256]{1,0:T(8,128)(2,1)S(1)}, bf16[16,11,128,128]{3,2,1,0:T(8,128)(2,1)S(1)}, bf16[256,256]{1,0:T(8,128)(2,1)S(1)}) custom-call(s32[2]{0:T(128)S(1)} %pad_add_fusion.here_ref, bf16[32,1,11,128,128]{4,3,2,1,0:T(8,128)(2,1)} %adj_hbm.3, bf16[64,256]{1,0:T(8,128)(2,1)S(1)} %constant_dynamic-update-slice_fusion.refs_0_, ...), custom_call_target="tpu_custom_call" | custom-call | flops 1703936000 | bytes 20971520 | tf_op jit(solution)/shard_map/pallas_call | solution.py:166
  71.6 4.2 %shard_map.83 = (bf16[2048,256]{1,0:T(8,128)(2,1)S(1)}, bf16[16512,256]{1,0:T(8,128)(2,1)S(1)}, bf16[16,11,128,128]{3,2,1,0:T(8,128)(2,1)S(1)}) custom-call(s32[2]{0:T(128)S(1)} %pad_add_fusion.here_ref, s32[32,1,11]{2,1,0:T(1,128)S(1)} %copy.12.index_ref, s32[32,1]{1,0:T(8,128)S(1)} %copy.13.count_ref, ...), custom_call_target="tpu_custom_call", output_to_operand_aliasing={{1}: (3, {})} | custom-call | flops 1500000000 | bytes 8388608 | tf_op jit(solution)/shard_map/pallas_call | solution.py:226
  75.9 3.6 %shard_map.84 = f32[2048,256]{1,0:T(8,128)S(1)} custom-call(s32[2]{0:T(128)S(1)} %pad_add_fusion.here_ref, s32[32,1,11]{2,1,0:T(1,128)S(1)} %copy.12.index_ref, s32[32,1]{1,0:T(8,128)S(1)} %copy.13.count_ref, bf16[16512,256]{1,0:T(8,128)(2,1)S(1)} %get-tuple-element.70.hidden, bf16[16,11,128,128]{3,2,1,0:T(8,128)(2,1)S(1)} %get-tuple-element.71.adj), custom_call_target="tpu_custom_call" | custom-call | flops 1500000000 | bytes 8388608 | tf_op jit(solution)/shard_map/pallas_call | solution.py:240
  79.6 2.8 %collective-permute-start.37 = (bf16[256,256]{1,0:T(8,128)(2,1)S(1)}, bf16[256,256]{1,0:T(8,128)(2,1)S(1)}, u32[]{:S(2)}, u32[]{:S(2)}) collective-permute-start(bf16[256,256]{1,0:T(8,128)(2,1)S(1)} %get-tuple-element.74), channel_id=1, source_target_pairs={{0,2},{1,3},{2,4},{3,5},{4,6},{5,7},{6,0},{7,1},{8,10},{9,11},{10,... | collective-permute-start | bytes 393224 | tf_op jit(solution)/shard_map/ppermute | solution.py:259
  84.6 6.0 %collective-permute-done.37 = bf16[256,256]{1,0:T(8,128)(2,1)S(1)} collective-permute-done((bf16[256,256]{1,0:T(8,128)(2,1)S(1)}, bf16[256,256]{1,0:T(8,128)(2,1)S(1)}, u32[]{:S(2)}, u32[]{:S(2)}) %collective-permute-start.37) | collective-permute-done | bytes 131104 | tf_op jit(solution)/shard_map/ppermute | solution.py:259
  92.1 1.8 %collective-permute-start.39 = (bf16[256,256]{1,0:T(8,128)(2,1)S(1)}, bf16[256,256]{1,0:T(8,128)(2,1)S(1)}, u32[]{:S(2)}, u32[]{:S(2)}) collective-permute-start(bf16[256,256]{1,0:T(8,128)(2,1)S(1)} %get-tuple-element.75), channel_id=1, source_target_pairs={{0,2},{1,3},{2,4},{3,5},{4,6},{5,7},{6,0},{7,1},{8,10},{9,11},{10,... | collective-permute-start | bytes 393224 | tf_op jit(solution)/shard_map/ppermute | solution.py:259
  93.9 7.7 %collective-permute-done.38 = bf16[256,256]{1,0:T(8,128)(2,1)S(1)} collective-permute-done((bf16[256,256]{1,0:T(8,128)(2,1)S(1)}, bf16[256,256]{1,0:T(8,128)(2,1)S(1)}, u32[]{:S(2)}, u32[]{:S(2)}) %collective-permute-start.38) | collective-permute-done | bytes 131104 | tf_op jit(solution)/shard_map/ppermute | solution.py:259
  102.3 2.0 %collective-permute-done.39 = bf16[256,256]{1,0:T(8,128)(2,1)S(1)} collective-permute-done((bf16[256,256]{1,0:T(8,128)(2,1)S(1)}, bf16[256,256]{1,0:T(8,128)(2,1)S(1)}, u32[]{:S(2)}, u32[]{:S(2)}) %collective-permute-start.39) | collective-permute-done | bytes 131104 | tf_op jit(solution)/shard_map/ppermute | solution.py:259
  104.4 3.8 %collective-permute-done.41 = bf16[256,256]{1,0:T(8,128)(2,1)S(1)} collective-permute-done((bf16[256,256]{1,0:T(8,128)(2,1)S(1)}, bf16[256,256]{1,0:T(8,128)(2,1)S(1)}, u32[]{:S(2)}, u32[]{:S(2)}) %collective-permute-start.41) | collective-permute-done | bytes 131104 | tf_op jit(solution)/shard_map/ppermute | solution.py:262
  (122 shorter events, 29.5 us)
Async XLA Ops:
  2.0 9.3 %collective-permute-start.7 = (bf16[512,256]{1,0:T(8,128)(2,1)S(1)}, bf16[512,256]{1,0:T(8,128)(2,1)S(1)}, u32[]{:S(2)}, u32[]{:S(2)}) collective-permute-start(bf16[512,256]{1,0:T(8,128)(2,1)S(1)} %multiply_convert_fusion.refs_4_), channel_id=1, source_target_pairs={{0,64},{8,72},{16,80},{24,88},{32,96},{40,104},{48,112},{56,120},{... | collective-permute-start | bytes 786440 | tf_op jit(solution)/shard_map/ppermute | solution.py:102
  11.3 8.4 %collective-permute-start.12 = (bf16[512,256]{1,0:T(8,128)(2,1)S(1)}, bf16[512,256]{1,0:T(8,128)(2,1)S(1)}, u32[]{:S(2)}, u32[]{:S(2)}) collective-permute-start(bf16[512,256]{1,0:T(8,128)(2,1)S(1)} %collective-permute-done.8.refs_9_), channel_id=1, source_target_pairs={{0,64},{8,72},{16,80},{24,88},{32,96},{40,104},{48,112},{56,120},{... | collective-permute-start | bytes 786440 | tf_op jit(solution)/shard_map/ppermute | solution.py:102
  23.1 8.8 %collective-permute-start.18 = (bf16[512,256]{1,0:T(8,128)(2,1)S(1)}, bf16[512,256]{1,0:T(8,128)(2,1)S(1)}, u32[]{:S(2)}, u32[]{:S(2)}) collective-permute-start(bf16[512,256]{1,0:T(8,128)(2,1)S(1)} %collective-permute-done.12.refs_13_), channel_id=1, source_target_pairs={{0,48},{8,56},{16,0},{24,8},{32,16},{40,24},{48,32},{56,40},{64,11... | collective-permute-start | bytes 786440 | tf_op jit(solution)/shard_map/ppermute | solution.py:102
  23.1 8.8 %collective-permute-start.15 = (bf16[512,256]{1,0:T(8,128)(2,1)S(1)}, bf16[512,256]{1,0:T(8,128)(2,1)S(1)}, u32[]{:S(2)}, u32[]{:S(2)}) collective-permute-start(bf16[512,256]{1,0:T(8,128)(2,1)S(1)} %collective-permute-done.8.refs_9_), channel_id=1, source_target_pairs={{0,192},{8,200},{16,208},{24,216},{32,224},{40,232},{48,240},{56,2... | collective-permute-start | bytes 786440 | tf_op jit(solution)/shard_map/ppermute | solution.py:102
  27.9 10.2 %collective-permute-start.19 = (bf16[512,256]{1,0:T(8,128)(2,1)S(1)}, bf16[512,256]{1,0:T(8,128)(2,1)S(1)}, u32[]{:S(2)}, u32[]{:S(2)}) collective-permute-start(bf16[512,256]{1,0:T(8,128)(2,1)S(1)} %collective-permute-done.7.refs_8_), channel_id=1, source_target_pairs={{0,16},{8,24},{16,32},{24,40},{32,48},{40,56},{48,0},{56,8},{64,80... | collective-permute-start | bytes 786440 | tf_op jit(solution)/shard_map/ppermute | solution.py:102
  31.9 9.8 %collective-permute-start.23 = (bf16[512,256]{1,0:T(8,128)(2,1)S(1)}, bf16[512,256]{1,0:T(8,128)(2,1)}, u32[]{:S(2)}, u32[]{:S(2)}) collective-permute-start(bf16[512,256]{1,0:T(8,128)(2,1)S(1)} %collective-permute-done.9.refs_10_), channel_id=1, source_target_pairs={{0,48},{8,56},{16,0},{24,8},{32,16},{40,24},{48,32},{56,40},{64,11... | collective-permute-start | bytes 786440 | tf_op jit(solution)/shard_map/ppermute | solution.py:102
  32.0 9.8 %collective-permute-start.20 = (bf16[512,256]{1,0:T(8,128)(2,1)S(1)}, bf16[512,256]{1,0:T(8,128)(2,1)S(1)}, u32[]{:S(2)}, u32[]{:S(2)}) collective-permute-start(bf16[512,256]{1,0:T(8,128)(2,1)S(1)} %collective-permute-done.11.refs_12_), channel_id=1, source_target_pairs={{0,192},{8,200},{16,208},{24,216},{32,224},{40,232},{48,240},{56,2... | collective-permute-start | bytes 786440 | tf_op jit(solution)/shard_map/ppermute | solution.py:102
  32.7 9.2 %collective-permute-start.22 = (bf16[512,256]{1,0:T(8,128)(2,1)S(1)}, bf16[512,256]{1,0:T(8,128)(2,1)S(1)}, u32[]{:S(2)}, u32[]{:S(2)}) collective-permute-start(bf16[512,256]{1,0:T(8,128)(2,1)S(1)} %collective-permute-done.10.refs_11_), channel_id=1, source_target_pairs={{0,8},{8,0},{16,24},{24,16},{32,40},{40,32},{48,56},{56,48},{64,72... | collective-permute-start | bytes 786440 | tf_op jit(solution)/shard_map/ppermute | solution.py:102
  41.7 9.2 %collective-permute-start.28 = (bf16[512,256]{1,0:T(8,128)(2,1)S(1)}, bf16[512,256]{1,0:T(8,128)(2,1)S(1)}, u32[]{:S(2)}, u32[]{:S(2)}) collective-permute-start(bf16[512,256]{1,0:T(8,128)(2,1)S(1)} %collective-permute-done.18.refs_19_), channel_id=1, source_target_pairs={{0,48},{8,56},{16,0},{24,8},{32,16},{40,24},{48,32},{56,40},{64,11... | collective-permute-start | bytes 786440 | tf_op jit(solution)/shard_map/ppermute | solution.py:102
  41.8 11.1 %collective-permute-start.25 = (bf16[512,256]{1,0:T(8,128)(2,1)}, bf16[512,256]{1,0:T(8,128)(2,1)S(1)}, u32[]{:S(2)}, u32[]{:S(2)}) collective-permute-start(bf16[512,256]{1,0:T(8,128)(2,1)} %collective-permute-done.14.refs_15_), channel_id=1, source_target_pairs={{0,192},{8,200},{16,208},{24,216},{32,224},{40,232},{48,240},{56,2... | collective-permute-start | bytes 786440 | tf_op jit(solution)/shard_map/ppermute | solution.py:102
  42.6 13.7 %collective-permute-start.27 = (bf16[512,256]{1,0:T(8,128)(2,1)}, bf16[512,256]{1,0:T(8,128)(2,1)}, u32[]{:S(2)}, u32[]{:S(2)}) collective-permute-start(bf16[512,256]{1,0:T(8,128)(2,1)} %collective-permute-done.14.refs_15_), channel_id=1, source_target_pairs={{0,8},{8,0},{16,24},{24,16},{32,40},{40,32},{48,56},{56,48},{64,72... | collective-permute-start | bytes 786440 | tf_op jit(solution)/shard_map/ppermute | solution.py:102
  44.6 12.6 %collective-permute-start.29 = (bf16[512,256]{1,0:T(8,128)(2,1)}, bf16[512,256]{1,0:T(8,128)(2,1)}, u32[]{:S(2)}, u32[]{:S(2)}) collective-permute-start(bf16[512,256]{1,0:T(8,128)(2,1)} %collective-permute-done.23.refs_24_), channel_id=1, source_target_pairs={{0,64},{8,72},{16,80},{24,88},{32,96},{40,104},{48,112},{56,120},{... | collective-permute-start | bytes 786440 | tf_op jit(solution)/shard_map/ppermute | solution.py:102
  46.1 12.1 %collective-permute-start.3 = (bf16[64,256]{1,0:T(8,128)(2,1)S(1)}, bf16[64,256]{1,0:T(8,128)(2,1)S(1)}, u32[]{:S(2)}, u32[]{:S(2)}) collective-permute-start(bf16[64,256]{1,0:T(8,128)(2,1)S(1)} %constant_dynamic-update-slice_fusion.refs_0_), channel_id=1, source_target_pairs={{0,6},{1,7},{2,0},{3,1},{4,2},{5,3},{6,4},{7,5},{8,14},{9,15},{10,... | collective-permute-start | bytes 98312 | tf_op jit(solution)/shard_map/ppermute | solution.py:112
  50.9 9.7 %collective-permute-start.2 = (bf16[64,256]{1,0:T(8,128)(2,1)S(1)}, bf16[64,256]{1,0:T(8,128)(2,1)S(1)}, u32[]{:S(2)}, u32[]{:S(2)}) collective-permute-start(bf16[64,256]{1,0:T(8,128)(2,1)S(1)} %constant_dynamic-update-slice_fusion.refs_0_), channel_id=1, source_target_pairs={{0,4},{1,5},{2,6},{3,7},{4,0},{5,1},{6,2},{7,3},{8,12},{9,13},{10,... | collective-permute-start | bytes 98312 | tf_op jit(solution)/shard_map/ppermute | solution.py:112
  52.9 10.9 %collective-permute-start.1 = (bf16[64,256]{1,0:T(8,128)(2,1)S(1)}, bf16[64,256]{1,0:T(8,128)(2,1)S(1)}, u32[]{:S(2)}, u32[]{:S(2)}) collective-permute-start(bf16[64,256]{1,0:T(8,128)(2,1)S(1)} %constant_dynamic-update-slice_fusion.refs_0_), channel_id=1, source_target_pairs={{0,2},{1,3},{2,4},{3,5},{4,6},{5,7},{6,0},{7,1},{8,10},{9,11},{10,... | collective-permute-start | bytes 98312 | tf_op jit(solution)/shard_map/ppermute | solution.py:112
  56.3 14.0 %collective-permute-start.33 = (bf16[512,256]{1,0:T(8,128)(2,1)}, bf16[512,256]{1,0:T(8,128)(2,1)S(1)}, u32[]{:S(2)}, u32[]{:S(2)}) collective-permute-start(bf16[512,256]{1,0:T(8,128)(2,1)} %copy-done.14), channel_id=1, source_target_pairs={{0,48},{8,56},{16,0},{24,8},{32,16},{40,24},{48,32},{56,40},{64,11... | collective-permute-start | bytes 786440 | tf_op jit(solution)/shard_map/ppermute | solution.py:102
  57.2 13.2 %collective-permute-start.32 = (bf16[512,256]{1,0:T(8,128)(2,1)S(1)}, bf16[512,256]{1,0:T(8,128)(2,1)S(1)}, u32[]{:S(2)}, u32[]{:S(2)}) collective-permute-start(bf16[512,256]{1,0:T(8,128)(2,1)S(1)} %collective-permute-done.11.refs_12_), channel_id=1, source_target_pairs={{0,8},{8,0},{16,24},{24,16},{32,40},{40,32},{48,56},{56,48},{64,72... | collective-permute-start | bytes 786440 | tf_op jit(solution)/shard_map/ppermute | solution.py:102
  58.2 12.2 %collective-permute-start.30 = (bf16[512,256]{1,0:T(8,128)(2,1)}, bf16[512,256]{1,0:T(8,128)(2,1)S(1)}, u32[]{:S(2)}, u32[]{:S(2)}) collective-permute-start(bf16[512,256]{1,0:T(8,128)(2,1)} %copy-done.16), channel_id=1, source_target_pairs={{0,16},{8,24},{16,32},{24,40},{32,48},{40,56},{48,0},{56,8},{64,80... | collective-permute-start | bytes 786440 | tf_op jit(solution)/shard_map/ppermute | solution.py:102
  60.6 9.8 %collective-permute-start.31 = (bf16[512,256]{1,0:T(8,128)(2,1)}, bf16[512,256]{1,0:T(8,128)(2,1)S(1)}, u32[]{:S(2)}, u32[]{:S(2)}) collective-permute-start(bf16[512,256]{1,0:T(8,128)(2,1)} %copy-done.16), channel_id=1, source_target_pairs={{0,192},{8,200},{16,208},{24,216},{32,224},{40,232},{48,240},{56,2... | collective-permute-start | bytes 786440 | tf_op jit(solution)/shard_map/ppermute | solution.py:102
  79.6 10.9 %collective-permute-start.37 = (bf16[256,256]{1,0:T(8,128)(2,1)S(1)}, bf16[256,256]{1,0:T(8,128)(2,1)S(1)}, u32[]{:S(2)}, u32[]{:S(2)}) collective-permute-start(bf16[256,256]{1,0:T(8,128)(2,1)S(1)} %get-tuple-element.74), channel_id=1, source_target_pairs={{0,2},{1,3},{2,4},{3,5},{4,6},{5,7},{6,0},{7,1},{8,10},{9,11},{10,... | collective-permute-start | bytes 393224 | tf_op jit(solution)/shard_map/ppermute | solution.py:259
  82.4 11.5 %collective-permute-start.36 = (bf16[256,256]{1,0:T(8,128)(2,1)S(1)}, bf16[256,256]{1,0:T(8,128)(2,1)S(1)}, u32[]{:S(2)}, u32[]{:S(2)}) collective-permute-start(bf16[256,256]{1,0:T(8,128)(2,1)S(1)} %get-tuple-element.73), channel_id=1, source_target_pairs={{0,6},{1,7},{2,0},{3,1},{4,2},{5,3},{6,4},{7,5},{8,14},{9,15},{10,... | collective-permute-start | bytes 393224 | tf_op jit(solution)/shard_map/ppermute | solution.py:262
  83.9 10.1 %collective-permute-start.40 = (bf16[256,256]{1,0:T(8,128)(2,1)S(1)}, bf16[256,256]{1,0:T(8,128)(2,1)S(1)}, u32[]{:S(2)}, u32[]{:S(2)}) collective-permute-start(bf16[256,256]{1,0:T(8,128)(2,1)S(1)} %get-tuple-element.76), channel_id=1, source_target_pairs={{0,6},{1,7},{2,0},{3,1},{4,2},{5,3},{6,4},{7,5},{8,14},{9,15},{10,... | collective-permute-start | bytes 393224 | tf_op jit(solution)/shard_map/ppermute | solution.py:262
  90.6 11.1 %collective-permute-start.38 = (bf16[256,256]{1,0:T(8,128)(2,1)S(1)}, bf16[256,256]{1,0:T(8,128)(2,1)S(1)}, u32[]{:S(2)}, u32[]{:S(2)}) collective-permute-start(bf16[256,256]{1,0:T(8,128)(2,1)S(1)} %fusion.7), channel_id=1, source_target_pairs={{0,2},{1,3},{2,4},{3,5},{4,6},{5,7},{6,0},{7,1},{8,10},{9,11},{10,... | collective-permute-start | bytes 393224 | tf_op jit(solution)/shard_map/ppermute | solution.py:259
  92.1 12.3 %collective-permute-start.39 = (bf16[256,256]{1,0:T(8,128)(2,1)S(1)}, bf16[256,256]{1,0:T(8,128)(2,1)S(1)}, u32[]{:S(2)}, u32[]{:S(2)}) collective-permute-start(bf16[256,256]{1,0:T(8,128)(2,1)S(1)} %get-tuple-element.75), channel_id=1, source_target_pairs={{0,2},{1,3},{2,4},{3,5},{4,6},{5,7},{6,0},{7,1},{8,10},{9,11},{10,... | collective-permute-start | bytes 393224 | tf_op jit(solution)/shard_map/ppermute | solution.py:259
  (42 other events, 809.9 us)

commit v4 on v3

--- a/solution.py
+++ b/solution.py
@@ -183,9 +183,9 @@
         table[shard] = n * PANEL
 
     def rows_at(block, m):
-        column = index_ref[block, 0, m]
+        column = index_ref[m, 0, block]
         start = table[lax.shift_right_logical(column, 2)] + (column & (KPER - 1)) * BLOCK
-        start = jnp.where(m < count_ref[block, 0], start, SHARDS * PANEL)
+        start = jnp.where(m < count_ref[0, block], start, SHARDS * PANEL)
         return hidden[pl.ds(pl.multiple_of(start, BLOCK), BLOCK), :]
 
     def total_of(block, at):
@@ -265,8 +265,10 @@
     first = lax.optimization_barrier([value.astype(jnp.bfloat16) for value in first])
     far_top, far_bottom = plus(first[0]), minus(first[1])
     near_bottom, near_top = plus(first[2]), minus(first[3])
-    chain_top = plus(part(1, 0) + far_top)
-    chain_bottom = minus(part(3, 1) + far_bottom)
+    chain_up = (part(1, 0) + far_top).astype(jnp.bfloat16)
+    chain_down = (part(3, 1) + far_bottom).astype(jnp.bfloat16)
+    chain_top, chain_bottom = plus(chain_up), minus(chain_down)
+    got, keep = lax.optimization_barrier((got, keep, chain_up, chain_down))[:2]
     top = part(0, 0) + near_top + chain_top
     bottom = part(0, 1) + near_bottom + chain_bottom
     return jnp.concatenate([top, bottom])
@@ -295,7 +297,7 @@
     blocks = pltpu.with_memory_space_constraint(adjacency_blocks, pltpu.HBM)
     pieces = [pltpu.with_memory_space_constraint(a, pltpu.HBM) for a, _ in soon]
     hidden, adj, full_weight = early(here, pairs, blocks, pieces)
-    tables = (here, block_index, block_counts)
+    tables = (here, block_index.transpose(2, 1, 0), block_counts.transpose(1, 0))
     send, hidden, adj = send_products(order, *tables, hidden, adj, blocks, full_weight, [a for a, _ in last])
     got = lax.ppermute(send, "col", col_perm(0, 1))
     keep = keep_products(order, *tables, hidden, adj)

time: 110 us -> 105 us (0.955)
  the two profiles are of different devices: /device:TPU:38 before, /device:TPU:1 now
where the time goes in v4:
time: 105 us
  starting transfers between devices  62.2 us (59%)
  waiting for transfers between devices  25.5 us (24%)
  Pallas kernels  13.3 us (13%)
  other arithmetic  2.32 us (2%)
    ppermute x31, starting transfers between devices, gather_rows(): last[link] = got = lax.ppermute(value, 'row', row_perm(axis, step))  32.9 us
    ppermute x31, waiting for transfers between devices, gather_rows(): last[link] = got = lax.ppermute(value, 'row', row_perm(axis, step))  11.3 us
    ppermute x1, starting transfers between devices, gather_weight(): lax.ppermute(weight, 'col', col_perm(0, 1))  7.84 us
    ppermute x3, waiting for transfers between devices, minus(): lax.ppermute(value.astype(jnp.bfloat16), 'col', col_perm(-1, 0))  7.74 us
    ppermute x3, starting transfers between devices, gather_weight(): lax.ppermute(pair, 'col', col_perm(d, 0))  7.36 us
    pallas_call x1, Pallas kernels, early(): pl.pallas_call(early_kernel, in_specs=[smem, anywhere] + [anywhere] * (le...  6.33 us
    ppermute x3, starting transfers between devices, minus(): lax.ppermute(value.astype(jnp.bfloat16), 'col', col_perm(-1, 0))  5.13 us
    ppermute x3, waiting for transfers between devices, plus(): lax.ppermute(value.astype(jnp.bfloat16), 'col', col_perm(1, 0))  4.86 us
  transfers between devices with their start and end apart: 42, of which 14 were waited for; matrix products, arithmetic and copies ran while one was open for 1% of the time, Pallas kernels for 9%

profile of v4, /device:TPU:1, one launch (start us, length us, event | category | flops | bytes accessed | tf_op | source)
XLA Modules:
  0.0 105.1 jit_solution(5731320347086163288)
XLA Ops:
  1.9 2.6 %collective-permute-start.8 = (bf16[512,256]{1,0:T(8,128)(2,1)S(1)}, bf16[512,256]{1,0:T(8,128)(2,1)S(1)}, u32[]{:S(2)}, u32[]{:S(2)}) collective-permute-start(bf16[512,256]{1,0:T(8,128)(2,1)S(1)} %multiply_convert_fusion.refs_4_), channel_id=1, source_target_pairs={{0,8},{8,0},{16,24},{24,16},{32,40},{40,32},{48,56},{56,48},{64,72... | collective-permute-start | bytes 786440 | tf_op jit(solution)/shard_map/ppermute | solution.py:102
  9.8 2.8 %collective-permute-done.7.refs_8_ = bf16[512,256]{1,0:T(8,128)(2,1)S(1)} collective-permute-done((bf16[512,256]{1,0:T(8,128)(2,1)S(1)}, bf16[512,256]{1,0:T(8,128)(2,1)S(1)}, u32[]{:S(2)}, u32[]{:S(2)}) %collective-permute-start.7) | collective-permute-done | bytes 262176 | tf_op jit(solution)/shard_map/ppermute | solution.py:102
  12.6 2.1 %collective-permute-done.5.refs_6_ = bf16[512,256]{1,0:T(8,128)(2,1)S(1)} collective-permute-done((bf16[512,256]{1,0:T(8,128)(2,1)S(1)}, bf16[512,256]{1,0:T(8,128)(2,1)S(1)}, u32[]{:S(2)}, u32[]{:S(2)}) %collective-permute-start.5) | collective-permute-done | bytes 262176 | tf_op jit(solution)/shard_map/ppermute | solution.py:102
  14.7 2.7 %collective-permute-start.9 = (bf16[512,256]{1,0:T(8,128)(2,1)S(1)}, bf16[512,256]{1,0:T(8,128)(2,1)S(1)}, u32[]{:S(2)}, u32[]{:S(2)}) collective-permute-start(bf16[512,256]{1,0:T(8,128)(2,1)S(1)} %collective-permute-done.7.refs_8_), channel_id=1, source_target_pairs={{0,48},{8,56},{16,0},{24,8},{32,16},{40,24},{48,32},{56,40},{64,11... | collective-permute-start | bytes 786440 | tf_op jit(solution)/shard_map/ppermute | solution.py:102
  21.4 2.7 %collective-permute-start.18 = (bf16[512,256]{1,0:T(8,128)(2,1)S(1)}, bf16[512,256]{1,0:T(8,128)(2,1)S(1)}, u32[]{:S(2)}, u32[]{:S(2)}) collective-permute-start(bf16[512,256]{1,0:T(8,128)(2,1)S(1)} %collective-permute-done.12.refs_13_), channel_id=1, source_target_pairs={{0,48},{8,56},{16,0},{24,8},{32,16},{40,24},{48,32},{56,40},{64,11... | collective-permute-start | bytes 786440 | tf_op jit(solution)/shard_map/ppermute | solution.py:102
  26.3 1.9 %collective-permute-done.14.refs_15_ = bf16[512,256]{1,0:T(8,128)(2,1)S(1)} collective-permute-done((bf16[512,256]{1,0:T(8,128)(2,1)S(1)}, bf16[512,256]{1,0:T(8,128)(2,1)S(1)}, u32[]{:S(2)}, u32[]{:S(2)}) %collective-permute-start.14) | collective-permute-done | bytes 262176 | tf_op jit(solution)/shard_map/ppermute | solution.py:102
  28.2 2.7 %collective-permute-start.23 = (bf16[512,256]{1,0:T(8,128)(2,1)S(1)}, bf16[512,256]{1,0:T(8,128)(2,1)}, u32[]{:S(2)}, u32[]{:S(2)}) collective-permute-start(bf16[512,256]{1,0:T(8,128)(2,1)S(1)} %collective-permute-done.9.refs_10_), channel_id=1, source_target_pairs={{0,48},{8,56},{16,0},{24,8},{32,16},{40,24},{48,32},{56,40},{64,11... | collective-permute-start | bytes 786440 | tf_op jit(solution)/shard_map/ppermute | solution.py:102
  32.7 1.9 %collective-permute-done.19.refs_20_ = bf16[512,256]{1,0:T(8,128)(2,1)S(1)} collective-permute-done((bf16[512,256]{1,0:T(8,128)(2,1)S(1)}, bf16[512,256]{1,0:T(8,128)(2,1)S(1)}, u32[]{:S(2)}, u32[]{:S(2)}) %collective-permute-start.19) | collective-permute-done | bytes 262176 | tf_op jit(solution)/shard_map/ppermute | solution.py:102
  34.6 3.0 %collective-permute-start.28 = (bf16[512,256]{1,0:T(8,128)(2,1)S(1)}, bf16[512,256]{1,0:T(8,128)(2,1)S(1)}, u32[]{:S(2)}, u32[]{:S(2)}) collective-permute-start(bf16[512,256]{1,0:T(8,128)(2,1)S(1)} %collective-permute-done.18.refs_19_), channel_id=1, source_target_pairs={{0,48},{8,56},{16,0},{24,8},{32,16},{40,24},{48,32},{56,40},{64,11... | collective-permute-start | bytes 786440 | tf_op jit(solution)/shard_map/ppermute | solution.py:102
  39.4 7.8 %collective-permute-start = (bf16[32,256]{1,0:T(8,128)(2,1)}, bf16[32,256]{1,0:T(8,128)(2,1)S(1)}, u32[]{:S(2)}, u32[]{:S(2)}) collective-permute-start(bf16[32,256]{1,0:T(8,128)(2,1)} %param.11), channel_id=1, source_target_pairs={{0,1},{1,0},{2,3},{3,2},{4,5},{5,4},{6,7},{7,6},{8,9},{9,8},{10,11... | collective-permute-start | bytes 49160 | tf_op jit(solution)/shard_map/ppermute | solution.py:111
  50.3 4.0 %collective-permute-start.3 = (bf16[64,256]{1,0:T(8,128)(2,1)S(1)}, bf16[64,256]{1,0:T(8,128)(2,1)S(1)}, u32[]{:S(2)}, u32[]{:S(2)}) collective-permute-start(bf16[64,256]{1,0:T(8,128)(2,1)S(1)} %constant_dynamic-update-slice_fusion.refs_0_), channel_id=1, source_target_pairs={{0,6},{1,7},{2,0},{3,1},{4,2},{5,3},{6,4},{7,5},{8,14},{9,15},{10,... | collective-permute-start | bytes 98312 | tf_op jit(solution)/shard_map/ppermute | solution.py:112
  55.5 2.2 %collective-permute-start.1 = (bf16[64,256]{1,0:T(8,128)(2,1)S(1)}, bf16[64,256]{1,0:T(8,128)(2,1)S(1)}, u32[]{:S(2)}, u32[]{:S(2)}) collective-permute-start(bf16[64,256]{1,0:T(8,128)(2,1)S(1)} %constant_dynamic-update-slice_fusion.refs_0_), channel_id=1, source_target_pairs={{0,2},{1,3},{2,4},{3,5},{4,6},{5,7},{6,0},{7,1},{8,10},{9,11},{10,... | collective-permute-start | bytes 98312 | tf_op jit(solution)/shard_map/ppermute | solution.py:112
  61.1 2.6 %collective-permute-start.31 = (bf16[512,256]{1,0:T(8,128)(2,1)}, bf16[512,256]{1,0:T(8,128)(2,1)S(1)}, u32[]{:S(2)}, u32[]{:S(2)}) collective-permute-start(bf16[512,256]{1,0:T(8,128)(2,1)} %copy-done.19), channel_id=1, source_target_pairs={{0,192},{8,200},{16,208},{24,216},{32,224},{40,232},{48,240},{56,2... | collective-permute-start | bytes 786440 | tf_op jit(solution)/shard_map/ppermute | solution.py:102
  64.0 6.3 %shard_map.82 = (bf16[16512,256]{1,0:T(8,128)(2,1)S(1)}, bf16[16,11,128,128]{3,2,1,0:T(8,128)(2,1)S(1)}, bf16[256,256]{1,0:T(8,128)(2,1)S(1)}) custom-call(s32[2]{0:T(128)S(1)} %pad_add_fusion.here_ref, bf16[32,1,11,128,128]{4,3,2,1,0:T(8,128)(2,1)} %adj_hbm.3, bf16[64,256]{1,0:T(8,128)(2,1)S(1)} %constant_dynamic-update-slice_fusion.refs_0_, ...), custom_call_target="tpu_custom_call" | custom-call | flops 1703936000 | bytes 20971520 | tf_op jit(solution)/shard_map/pallas_call | solution.py:166
  70.4 3.7 %shard_map.83 = (bf16[2048,256]{1,0:T(8,128)(2,1)S(1)}, bf16[16512,256]{1,0:T(8,128)(2,1)S(1)}, bf16[16,11,128,128]{3,2,1,0:T(8,128)(2,1)S(1)}) custom-call(s32[2]{0:T(128)S(1)} %pad_add_fusion.here_ref, s32[11,1,32]{2,1,0:T(1,128)S(1)} %bitcast.5, s32[1,32]{1,0:T(1,128)S(1)} %bitcast.7, ...), custom_call_target="tpu_custom_call", output_to_operand_aliasing={{1}: (3, {})} | custom-call | flops 1500000000 | bytes 8388608 | tf_op jit(solution)/shard_map/pallas_call | solution.py:226
  74.1 4.1 %collective-permute-start.35 = (bf16[2048,256]{1,0:T(8,128)(2,1)S(1)}, bf16[2048,256]{1,0:T(8,128)(2,1)S(1)}, u32[]{:S(2)}, u32[]{:S(2)}) collective-permute-start(bf16[2048,256]{1,0:T(8,128)(2,1)S(1)} %get-tuple-element.72), channel_id=1, source_target_pairs={{0,1},{1,0},{2,3},{3,2},{4,5},{5,4},{6,7},{7,6},{8,9},{9,8},{10,11... | collective-permute-start | bytes 3145736 | tf_op jit(solution)/shard_map/ppermute | solution.py:302
  78.2 3.2 %shard_map.84 = f32[2048,256]{1,0:T(8,128)S(1)} custom-call(s32[2]{0:T(128)S(1)} %pad_add_fusion.here_ref, s32[11,1,32]{2,1,0:T(1,128)S(1)} %bitcast.6, s32[1,32]{1,0:T(1,128)S(1)} %bitcast.8, bf16[16512,256]{1,0:T(8,128)(2,1)S(1)} %get-tuple-element.73.hidden, bf16[16,11,128,128]{3,2,1,0:T(8,128)(2,1)S(1)} %get-tuple-element.74.adj), custom_call_target="tpu_custom_call" | custom-call | flops 1500000000 | bytes 8388608 | tf_op jit(solution)/shard_map/pallas_call | solution.py:240
  82.7 2.5 %collective-permute-start.37 = (bf16[256,256]{1,0:T(8,128)(2,1)S(1)}, bf16[256,256]{1,0:T(8,128)(2,1)S(1)}, u32[]{:S(2)}, u32[]{:S(2)}) collective-permute-start(bf16[256,256]{1,0:T(8,128)(2,1)S(1)} %get-tuple-element.76), channel_id=1, source_target_pairs={{0,6},{1,7},{2,0},{3,1},{4,2},{5,3},{6,4},{7,5},{8,14},{9,15},{10,... | collective-permute-start | bytes 393224 | tf_op jit(solution)/shard_map/ppermute | solution.py:262
  85.5 2.1 %collective-permute-start.40 = (bf16[256,256]{1,0:T(8,128)(2,1)S(1)}, bf16[256,256]{1,0:T(8,128)(2,1)S(1)}, u32[]{:S(2)}, u32[]{:S(2)}) collective-permute-start(bf16[256,256]{1,0:T(8,128)(2,1)S(1)} %get-tuple-element.80), channel_id=1, source_target_pairs={{0,2},{1,3},{2,4},{3,5},{4,6},{5,7},{6,0},{7,1},{8,10},{9,11},{10,... | collective-permute-start | bytes 393224 | tf_op jit(solution)/shard_map/ppermute | solution.py:259
  87.6 2.3 %collective-permute-done.36 = bf16[256,256]{1,0:T(8,128)(2,1)S(1)} collective-permute-done((bf16[256,256]{1,0:T(8,128)(2,1)S(1)}, bf16[256,256]{1,0:T(8,128)(2,1)S(1)}, u32[]{:S(2)}, u32[]{:S(2)}) %collective-permute-start.36) | collective-permute-done | bytes 131104 | tf_op jit(solution)/shard_map/ppermute | solution.py:259
  89.9 4.3 %collective-permute-done.37 = bf16[256,256]{1,0:T(8,128)(2,1)S(1)} collective-permute-done((bf16[256,256]{1,0:T(8,128)(2,1)S(1)}, bf16[256,256]{1,0:T(8,128)(2,1)S(1)}, u32[]{:S(2)}, u32[]{:S(2)}) %collective-permute-start.37) | collective-permute-done | bytes 131104 | tf_op jit(solution)/shard_map/ppermute | solution.py:262
  95.9 2.4 %collective-permute-start.41 = (bf16[256,256]{1,0:T(8,128)(2,1)S(1)}, bf16[256,256]{1,0:T(8,128)(2,1)S(1)}, u32[]{:S(2)}, u32[]{:S(2)}) collective-permute-start(bf16[256,256]{1,0:T(8,128)(2,1)S(1)} %get-tuple-element.84), channel_id=1, source_target_pairs={{0,6},{1,7},{2,0},{3,1},{4,2},{5,3},{6,4},{7,5},{8,14},{9,15},{10,... | collective-permute-start | bytes 393224 | tf_op jit(solution)/shard_map/ppermute | solution.py:262
  98.3 2.5 %collective-permute-done.39 = bf16[256,256]{1,0:T(8,128)(2,1)S(1)} collective-permute-done((bf16[256,256]{1,0:T(8,128)(2,1)S(1)}, bf16[256,256]{1,0:T(8,128)(2,1)S(1)}, u32[]{:S(2)}, u32[]{:S(2)}) %collective-permute-start.39) | collective-permute-done | bytes 131104 | tf_op jit(solution)/shard_map/ppermute | solution.py:259
  100.8 3.4 %collective-permute-done.41 = bf16[256,256]{1,0:T(8,128)(2,1)S(1)} collective-permute-done((bf16[256,256]{1,0:T(8,128)(2,1)S(1)}, bf16[256,256]{1,0:T(8,128)(2,1)S(1)}, u32[]{:S(2)}, u32[]{:S(2)}) %collective-permute-start.41) | collective-permute-done | bytes 131104 | tf_op jit(solution)/shard_map/ppermute | solution.py:262
  (125 shorter events, 28.3 us)
Async XLA Ops:
  1.9 8.0 %collective-permute-start.8 = (bf16[512,256]{1,0:T(8,128)(2,1)S(1)}, bf16[512,256]{1,0:T(8,128)(2,1)S(1)}, u32[]{:S(2)}, u32[]{:S(2)}) collective-permute-start(bf16[512,256]{1,0:T(8,128)(2,1)S(1)} %multiply_convert_fusion.refs_4_), channel_id=1, source_target_pairs={{0,8},{8,0},{16,24},{24,16},{32,40},{40,32},{48,56},{56,48},{64,72... | collective-permute-start | bytes 786440 | tf_op jit(solution)/shard_map/ppermute | solution.py:102
  4.4 8.2 %collective-permute-start.7 = (bf16[512,256]{1,0:T(8,128)(2,1)S(1)}, bf16[512,256]{1,0:T(8,128)(2,1)S(1)}, u32[]{:S(2)}, u32[]{:S(2)}) collective-permute-start(bf16[512,256]{1,0:T(8,128)(2,1)S(1)} %multiply_convert_fusion.refs_4_), channel_id=1, source_target_pairs={{0,64},{8,72},{16,80},{24,88},{32,96},{40,104},{48,112},{56,120},{... | collective-permute-start | bytes 786440 | tf_op jit(solution)/shard_map/ppermute | solution.py:102
  7.1 7.6 %collective-permute-start.5 = (bf16[512,256]{1,0:T(8,128)(2,1)S(1)}, bf16[512,256]{1,0:T(8,128)(2,1)S(1)}, u32[]{:S(2)}, u32[]{:S(2)}) collective-permute-start(bf16[512,256]{1,0:T(8,128)(2,1)S(1)} %multiply_convert_fusion.refs_4_), channel_id=1, source_target_pairs={{0,16},{8,24},{16,32},{24,40},{32,48},{40,56},{48,0},{56,8},{64,80... | collective-permute-start | bytes 786440 | tf_op jit(solution)/shard_map/ppermute | solution.py:102
  12.6 7.2 %collective-permute-start.12 = (bf16[512,256]{1,0:T(8,128)(2,1)S(1)}, bf16[512,256]{1,0:T(8,128)(2,1)S(1)}, u32[]{:S(2)}, u32[]{:S(2)}) collective-permute-start(bf16[512,256]{1,0:T(8,128)(2,1)S(1)} %collective-permute-done.8.refs_9_), channel_id=1, source_target_pairs={{0,64},{8,72},{16,80},{24,88},{32,96},{40,104},{48,112},{56,120},{... | collective-permute-start | bytes 786440 | tf_op jit(solution)/shard_map/ppermute | solution.py:102
  32.2 7.1 %collective-permute-start.22 = (bf16[512,256]{1,0:T(8,128)(2,1)S(1)}, bf16[512,256]{1,0:T(8,128)(2,1)S(1)}, u32[]{:S(2)}, u32[]{:S(2)}) collective-permute-start(bf16[512,256]{1,0:T(8,128)(2,1)S(1)} %collective-permute-done.10.refs_11_), channel_id=1, source_target_pairs={{0,8},{8,0},{16,24},{24,16},{32,40},{40,32},{48,56},{56,48},{64,72... | collective-permute-start | bytes 786440 | tf_op jit(solution)/shard_map/ppermute | solution.py:102
  32.7 14.5 %collective-permute-start.26 = (bf16[512,256]{1,0:T(8,128)(2,1)S(1)}, bf16[512,256]{1,0:T(8,128)(2,1)S(1)}, u32[]{:S(2)}, u32[]{:S(2)}) collective-permute-start(bf16[512,256]{1,0:T(8,128)(2,1)S(1)} %collective-permute-done.13.refs_14_), channel_id=1, source_target_pairs={{0,64},{8,72},{16,80},{24,88},{32,96},{40,104},{48,112},{56,120},{... | collective-permute-start | bytes 786440 | tf_op jit(solution)/shard_map/ppermute | solution.py:102
  34.6 15.7 %collective-permute-start.24 = (bf16[512,256]{1,0:T(8,128)(2,1)S(1)}, bf16[512,256]{1,0:T(8,128)(2,1)S(1)}, u32[]{:S(2)}, u32[]{:S(2)}) collective-permute-start(bf16[512,256]{1,0:T(8,128)(2,1)S(1)} %collective-permute-done.16.refs_17_), channel_id=1, source_target_pairs={{0,16},{8,24},{16,32},{24,40},{32,48},{40,56},{48,0},{56,8},{64,80... | collective-permute-start | bytes 786440 | tf_op jit(solution)/shard_map/ppermute | solution.py:102
  34.6 19.7 %collective-permute-start.28 = (bf16[512,256]{1,0:T(8,128)(2,1)S(1)}, bf16[512,256]{1,0:T(8,128)(2,1)S(1)}, u32[]{:S(2)}, u32[]{:S(2)}) collective-permute-start(bf16[512,256]{1,0:T(8,128)(2,1)S(1)} %collective-permute-done.18.refs_19_), channel_id=1, source_target_pairs={{0,48},{8,56},{16,0},{24,8},{32,16},{40,24},{48,32},{56,40},{64,11... | collective-permute-start | bytes 786440 | tf_op jit(solution)/shard_map/ppermute | solution.py:102
  37.6 17.9 %collective-permute-start.25 = (bf16[512,256]{1,0:T(8,128)(2,1)S(1)}, bf16[512,256]{1,0:T(8,128)(2,1)S(1)}, u32[]{:S(2)}, u32[]{:S(2)}) collective-permute-start(bf16[512,256]{1,0:T(8,128)(2,1)S(1)} %collective-permute-done.14.refs_15_), channel_id=1, source_target_pairs={{0,192},{8,200},{16,208},{24,216},{32,224},{40,232},{48,240},{56,2... | collective-permute-start | bytes 786440 | tf_op jit(solution)/shard_map/ppermute | solution.py:102
  39.4 8.9 %collective-permute-start = (bf16[32,256]{1,0:T(8,128)(2,1)}, bf16[32,256]{1,0:T(8,128)(2,1)S(1)}, u32[]{:S(2)}, u32[]{:S(2)}) collective-permute-start(bf16[32,256]{1,0:T(8,128)(2,1)} %param.11), channel_id=1, source_target_pairs={{0,1},{1,0},{2,3},{3,2},{4,5},{5,4},{6,7},{7,6},{8,9},{9,8},{10,11... | collective-permute-start | bytes 49160 | tf_op jit(solution)/shard_map/ppermute | solution.py:111
  47.2 10.5 %collective-permute-start.27 = (bf16[512,256]{1,0:T(8,128)(2,1)S(1)}, bf16[512,256]{1,0:T(8,128)(2,1)}, u32[]{:S(2)}, u32[]{:S(2)}) collective-permute-start(bf16[512,256]{1,0:T(8,128)(2,1)S(1)} %collective-permute-done.14.refs_15_), channel_id=1, source_target_pairs={{0,8},{8,0},{16,24},{24,16},{32,40},{40,32},{48,56},{56,48},{64,72... | collective-permute-start | bytes 786440 | tf_op jit(solution)/shard_map/ppermute | solution.py:102
  48.3 9.5 %collective-permute-start.29 = (bf16[512,256]{1,0:T(8,128)(2,1)}, bf16[512,256]{1,0:T(8,128)(2,1)}, u32[]{:S(2)}, u32[]{:S(2)}) collective-permute-start(bf16[512,256]{1,0:T(8,128)(2,1)} %collective-permute-done.23.refs_24_), channel_id=1, source_target_pairs={{0,64},{8,72},{16,80},{24,88},{32,96},{40,104},{48,112},{56,120},{... | collective-permute-start | bytes 786440 | tf_op jit(solution)/shard_map/ppermute | solution.py:102
  50.3 8.3 %collective-permute-start.3 = (bf16[64,256]{1,0:T(8,128)(2,1)S(1)}, bf16[64,256]{1,0:T(8,128)(2,1)S(1)}, u32[]{:S(2)}, u32[]{:S(2)}) collective-permute-start(bf16[64,256]{1,0:T(8,128)(2,1)S(1)} %constant_dynamic-update-slice_fusion.refs_0_), channel_id=1, source_target_pairs={{0,6},{1,7},{2,0},{3,1},{4,2},{5,3},{6,4},{7,5},{8,14},{9,15},{10,... | collective-permute-start | bytes 98312 | tf_op jit(solution)/shard_map/ppermute | solution.py:112
  55.5 8.2 %collective-permute-start.1 = (bf16[64,256]{1,0:T(8,128)(2,1)S(1)}, bf16[64,256]{1,0:T(8,128)(2,1)S(1)}, u32[]{:S(2)}, u32[]{:S(2)}) collective-permute-start(bf16[64,256]{1,0:T(8,128)(2,1)S(1)} %constant_dynamic-update-slice_fusion.refs_0_), channel_id=1, source_target_pairs={{0,2},{1,3},{2,4},{3,5},{4,6},{5,7},{6,0},{7,1},{8,10},{9,11},{10,... | collective-permute-start | bytes 98312 | tf_op jit(solution)/shard_map/ppermute | solution.py:112
  57.7 12.6 %collective-permute-start.33 = (bf16[512,256]{1,0:T(8,128)(2,1)}, bf16[512,256]{1,0:T(8,128)(2,1)S(1)}, u32[]{:S(2)}, u32[]{:S(2)}) collective-permute-start(bf16[512,256]{1,0:T(8,128)(2,1)} %copy-done.17), channel_id=1, source_target_pairs={{0,48},{8,56},{16,0},{24,8},{32,16},{40,24},{48,32},{56,40},{64,11... | collective-permute-start | bytes 786440 | tf_op jit(solution)/shard_map/ppermute | solution.py:102
  57.8 12.5 %collective-permute-start.32 = (bf16[512,256]{1,0:T(8,128)(2,1)S(1)}, bf16[512,256]{1,0:T(8,128)(2,1)S(1)}, u32[]{:S(2)}, u32[]{:S(2)}) collective-permute-start(bf16[512,256]{1,0:T(8,128)(2,1)S(1)} %collective-permute-done.11.refs_12_), channel_id=1, source_target_pairs={{0,8},{8,0},{16,24},{24,16},{32,40},{40,32},{48,56},{56,48},{64,72... | collective-permute-start | bytes 786440 | tf_op jit(solution)/shard_map/ppermute | solution.py:102
  58.6 11.7 %collective-permute-start.30 = (bf16[512,256]{1,0:T(8,128)(2,1)}, bf16[512,256]{1,0:T(8,128)(2,1)S(1)}, u32[]{:S(2)}, u32[]{:S(2)}) collective-permute-start(bf16[512,256]{1,0:T(8,128)(2,1)} %copy-done.19), channel_id=1, source_target_pairs={{0,16},{8,24},{16,32},{24,40},{32,48},{40,56},{48,0},{56,8},{64,80... | collective-permute-start | bytes 786440 | tf_op jit(solution)/shard_map/ppermute | solution.py:102
  61.1 9.2 %collective-permute-start.31 = (bf16[512,256]{1,0:T(8,128)(2,1)}, bf16[512,256]{1,0:T(8,128)(2,1)S(1)}, u32[]{:S(2)}, u32[]{:S(2)}) collective-permute-start(bf16[512,256]{1,0:T(8,128)(2,1)} %copy-done.19), channel_id=1, source_target_pairs={{0,192},{8,200},{16,208},{24,216},{32,224},{40,232},{48,240},{56,2... | collective-permute-start | bytes 786440 | tf_op jit(solution)/shard_map/ppermute | solution.py:102
  74.1 7.3 %collective-permute-start.35 = (bf16[2048,256]{1,0:T(8,128)(2,1)S(1)}, bf16[2048,256]{1,0:T(8,128)(2,1)S(1)}, u32[]{:S(2)}, u32[]{:S(2)}) collective-permute-start(bf16[2048,256]{1,0:T(8,128)(2,1)S(1)} %get-tuple-element.72), channel_id=1, source_target_pairs={{0,1},{1,0},{2,3},{3,2},{4,5},{5,4},{6,7},{7,6},{8,9},{9,8},{10,11... | collective-permute-start | bytes 3145736 | tf_op jit(solution)/shard_map/ppermute | solution.py:302
  81.6 8.3 %collective-permute-start.36 = (bf16[256,256]{1,0:T(8,128)(2,1)S(1)}, bf16[256,256]{1,0:T(8,128)(2,1)S(1)}, u32[]{:S(2)}, u32[]{:S(2)}) collective-permute-start(bf16[256,256]{1,0:T(8,128)(2,1)S(1)} %get-tuple-element.75), channel_id=1, source_target_pairs={{0,2},{1,3},{2,4},{3,5},{4,6},{5,7},{6,0},{7,1},{8,10},{9,11},{10,... | collective-permute-start | bytes 393224 | tf_op jit(solution)/shard_map/ppermute | solution.py:259
  82.7 11.5 %collective-permute-start.37 = (bf16[256,256]{1,0:T(8,128)(2,1)S(1)}, bf16[256,256]{1,0:T(8,128)(2,1)S(1)}, u32[]{:S(2)}, u32[]{:S(2)}) collective-permute-start(bf16[256,256]{1,0:T(8,128)(2,1)S(1)} %get-tuple-element.76), channel_id=1, source_target_pairs={{0,6},{1,7},{2,0},{3,1},{4,2},{5,3},{6,4},{7,5},{8,14},{9,15},{10,... | collective-permute-start | bytes 393224 | tf_op jit(solution)/shard_map/ppermute | solution.py:262
  85.2 13.0 %collective-permute-start.38 = (bf16[256,256]{1,0:T(8,128)(2,1)S(1)}, bf16[256,256]{1,0:T(8,128)(2,1)S(1)}, u32[]{:S(2)}, u32[]{:S(2)}) collective-permute-start(bf16[256,256]{1,0:T(8,128)(2,1)S(1)} %get-tuple-element.79), channel_id=1, source_target_pairs={{0,6},{1,7},{2,0},{3,1},{4,2},{5,3},{6,4},{7,5},{8,14},{9,15},{10,... | collective-permute-start | bytes 393224 | tf_op jit(solution)/shard_map/ppermute | solution.py:262
  85.5 12.8 %collective-permute-start.40 = (bf16[256,256]{1,0:T(8,128)(2,1)S(1)}, bf16[256,256]{1,0:T(8,128)(2,1)S(1)}, u32[]{:S(2)}, u32[]{:S(2)}) collective-permute-start(bf16[256,256]{1,0:T(8,128)(2,1)S(1)} %get-tuple-element.80), channel_id=1, source_target_pairs={{0,2},{1,3},{2,4},{3,5},{4,6},{5,7},{6,0},{7,1},{8,10},{9,11},{10,... | collective-permute-start | bytes 393224 | tf_op jit(solution)/shard_map/ppermute | solution.py:259
  95.9 8.4 %collective-permute-start.41 = (bf16[256,256]{1,0:T(8,128)(2,1)S(1)}, bf16[256,256]{1,0:T(8,128)(2,1)S(1)}, u32[]{:S(2)}, u32[]{:S(2)}) collective-permute-start(bf16[256,256]{1,0:T(8,128)(2,1)S(1)} %get-tuple-element.84), channel_id=1, source_target_pairs={{0,6},{1,7},{2,0},{3,1},{4,2},{5,3},{6,4},{7,5},{8,14},{9,15},{10,... | collective-permute-start | bytes 393224 | tf_op jit(solution)/shard_map/ppermute | solution.py:262
  (45 other events, 879.7 us)
